TPU v7x, 32 devices: a whole 2x2x4 slice. The times are simulated.
32 devices in a mesh: grp: 4 (over x, core), seq: 8 (over z, y).
Axes of the slice: x: 2, y: 2, z: 4, core: 2. Of those that a mesh axis runs over, the one named last changes fastest.
Arguments:
- queries: bfloat16 [4096, 512], P(('grp', 'seq')), may hold values from -4.5 to 5.5
- key_vectors: bfloat16 [4096, 512], P(('grp', 'seq')), may hold values from -4.5 to 5.5
- value_vectors: bfloat16 [4096, 1024], P(('grp', 'seq')), may hold values from -6 to 6
- input_gate: float32 [4, 4096], P(None, ('grp', 'seq')), may hold values from -4 to 114
- forget_gate: float32 [4, 4096], P(None, ('grp', 'seq')), may hold values from -3 to 25
Outputs:
- hidden_states: bfloat16 [4096, 1024], P(('grp', 'seq'))
All inputs are finite; a program needn't handle non-finite values.
Results may differ from a plain program's by a relative error of at most 0.028.
Values sent between devices are 32-bit elements; how exact they have to be, the bound alone decides.
No kernel may reach another device: no remote copies, remote signals or barrier semaphores. Data moves between devices by JAX's collectives and lax.ppermute only.
A program may use at most 64 MiB of HBM per device.

v0:
```python
import functools

import jax
import jax.numpy as jnp
from jax import lax
from jax.experimental import pallas as pl
from jax.experimental.pallas import tpu as pltpu
from jax.sharding import PartitionSpec as P

floor_value = -1e30
LANES = 128
AXES = ("grp", "seq")


def split_two(x):
    high = x.astype(jnp.bfloat16)
    low = (x - high.astype(jnp.float32)).astype(jnp.bfloat16)
    return high, low


def split_three(x):
    high = x.astype(jnp.bfloat16)
    rest = x - high.astype(jnp.float32)
    mid = rest.astype(jnp.bfloat16)
    low = (rest - mid.astype(jnp.float32)).astype(jnp.bfloat16)
    return high, mid, low


def dot(a, b):
    return jnp.dot(a, b, preferred_element_type=jnp.float32)


def dot_last(a, b):
    return lax.dot_general(a, b, (((1,), (1,)), ((), ())), preferred_element_type=jnp.float32)


def log_forget(forget):
    return jnp.minimum(forget, 0.0) - jnp.log1p(jnp.exp(-jnp.abs(forget)))


def triangle(length, lower):
    rows = lax.broadcasted_iota(jnp.int32, (length, length), 0)
    cols = lax.broadcasted_iota(jnp.int32, (length, length), 1)
    return rows >= cols if lower else rows <= cols


def cumulative_rows(logf):
    ones = triangle(logf.shape[1], False).astype(jnp.bfloat16)
    high, mid, low = split_three(logf)
    return (dot(low, ones) + dot(mid, ones)) + dot(high, ones)


def cumulative_columns(logf):
    ones = triangle(logf.shape[1], True).astype(jnp.bfloat16)
    high, mid, low = split_three(logf)
    return (dot_last(ones, low) + dot_last(ones, mid)) + dot_last(ones, high)


TAIL = 8
VECTOR, TOP, DECAY = range(3)


def member(quad):
    return lax.rem(lax.axis_index(AXES[1]), quad)


def distances(quad, side):
    order = [0, 1, quad - 1, *range(2, quad - 1)]
    bits = quad.bit_length() - 1
    if side:
        return order
    return [sum(((step >> bit) & 1) << (bits - 1 - bit) for bit in range(bits)) for step in order]


def partners(quad):
    even = (lax.axis_index(AXES[0]) & 1) == 0
    return [
        member(quad) ^ jnp.where(even, one, other)
        for one, other in zip(distances(quad, 0), distances(quad, 1))
    ]


def tail_rows(vector, top, decay):
    rest = jnp.zeros((TAIL - 3, vector.shape[1]), jnp.float32)
    return jnp.concatenate([vector, top, decay, rest], axis=0)


def tail_row(ref, row):
    first = ref.shape[0] - TAIL + row
    return ref[first : first + 1, :]


def load(ref):
    return (ref[0 : ref.shape[0] - TAIL, :], *(tail_row(ref, row) for row in range(3)))


def store(ref, state):
    matrix, *tail = state
    ref[0 : matrix.shape[0], :] = matrix
    ref[matrix.shape[0] :, :] = tail_rows(*tail)


def join(earlier, later):
    early_matrix, early_vector, early_top, early_decay = earlier
    late_matrix, late_vector, late_top, late_decay = later
    moved = early_top + late_decay
    joined = jnp.maximum(moved, late_top)
    early_weight, late_weight = jnp.exp(moved - joined), jnp.exp(late_top - joined)
    return (
        early_weight * early_matrix + late_weight * late_matrix,
        early_weight * early_vector + late_weight * late_vector,
        joined,
        early_decay + late_decay,
    )


def choose(condition, one, other):
    return jax.tree.map(lambda a, b: jnp.where(condition, a, b), one, other)


def nothing(like):
    matrix, vector, top, decay = like
    zero = jnp.zeros_like(decay)
    return jnp.zeros_like(matrix), jnp.zeros_like(vector), zero + floor_value, zero


def state_kernel(k_hbm, v_hbm, in_hbm, fo_hbm, *refs):
    *out_refs, k_ref, v_ref, in_ref, fo_ref, scalar_ref, arrived = refs
    copies = [
        pltpu.make_async_copy(source, target, arrived.at[place])
        for place, (source, target) in enumerate(
            ((fo_hbm, fo_ref), (in_hbm, in_ref), (k_hbm, k_ref), (v_hbm, v_ref))
        )
    ]
    for copy in copies:
        copy.start()
    heads, length = in_ref.shape
    key_dim = k_ref.shape[1] // heads
    value_dim = v_ref.shape[1] // heads
    parts = value_dim // LANES
    copies[0].wait()
    cumul = cumulative_rows(log_forget(fo_ref[...]))
    copies[1].wait()
    level = in_ref[...] - cumul
    level_top = jnp.max(level, axis=1, keepdims=True)
    decay = cumul[:, length - 1 : length]
    scalar_ref[0] = jnp.exp(level - level_top)
    scalar_ref[1] = jnp.broadcast_to(decay + level_top, (heads, length))
    scalar_ref[2] = jnp.broadcast_to(decay, (heads, length))
    copies[2].wait()
    copies[3].wait()
    for head, out_ref in zip(partners(heads), out_refs):
        keys = k_ref[:, pl.ds(pl.multiple_of(head * key_dim, LANES), key_dim)]
        values = v_ref[:, pl.ds(pl.multiple_of(head * value_dim, LANES), value_dim)]
        row, top, decay = (scalar_ref[place, pl.ds(head, 1), :] for place in range(3))
        high, low = split_two(keys.astype(jnp.float32).T * row)
        matrix = dot(
            jnp.concatenate([high, low], axis=1), jnp.concatenate([values, values], axis=0)
        )
        for part in range(parts):
            out_ref[part * key_dim : (part + 1) * key_dim, :] = matrix[
                :, part * LANES : (part + 1) * LANES
            ]
        high, mid, low = split_three(row)
        vector = (dot(low, keys) + dot(mid, keys)) + dot(high, keys)
        out_ref[parts * key_dim :, :] = tail_rows(vector, top, decay)


def read_scalars(refs, scalar_ref, places):
    for place, ref in zip(places, refs):
        scalar_ref[0, pl.ds(place, 1), :] = tail_row(ref, TOP)
        scalar_ref[1, pl.ds(place, 1), :] = tail_row(ref, DECAY)
    count = len(refs)
    tops = [scalar_ref[0, place : place + 1, :] for place in range(count)]
    decays = [scalar_ref[1, place : place + 1, :] for place in range(count)]
    return tops, decays


def weights_of(tops, decays):
    moved, total = [], jnp.zeros_like(decays[0])
    for top, decay in zip(reversed(tops), reversed(decays)):
        moved.append(top + total)
        total = total + decay
    moved.reverse()
    joined = functools.reduce(jnp.maximum, moved)
    return [jnp.exp(top - joined) for top in moved], joined, total


def weighted_sum(weights, states):
    matrix, vector = 0.0, 0.0
    for weight, state in zip(weights, states):
        matrix = matrix + weight * state[0]
        vector = vector + weight * state[1]
    return matrix, vector


def quad_kernel(*refs):
    *refs, out_ref, scalar_ref = refs
    places = partners(len(refs))
    weights, top, decay = weights_of(*read_scalars(refs, scalar_ref, places))
    for place, weight in enumerate(weights):
        scalar_ref[0, place : place + 1, :] = weight
    weights = [scalar_ref[0, pl.ds(place, 1), :] for place in places]
    store(out_ref, (*weighted_sum(weights, [load(ref) for ref in refs]), top, decay))


def later_side(axis, bit):
    return (lax.axis_index(axis) & bit) != 0


def butterfly_kernel(axis, bit, *refs):
    total_ref, other_ref, *before_refs, out_total, out_before = refs
    is_later = later_side(axis, bit)
    total, other = load(total_ref), load(other_ref)
    before = load(before_refs[0]) if before_refs else nothing(total)
    store(out_total, join(choose(is_later, other, total), choose(is_later, total, other)))
    store(out_before, choose(is_later, join(other, before), before))


def gather_kernel(axis, bit, own_ref, other_ref, out_ref):
    is_later = later_side(axis, bit)
    count = out_ref.shape[0] // 2
    for place in range(count):
        own = own_ref[place] if own_ref.ndim == 3 else own_ref[...]
        other = other_ref[place] if other_ref.ndim == 3 else other_ref[...]
        out_ref[place] = jnp.where(is_later, other, own)
        out_ref[count + place] = jnp.where(is_later, own, other)


def prefix_kernel(quad, own_ref, other_ref, within_ref, *refs):
    *refs, scalar_ref, weight_ref = refs
    pieces, out_refs = refs[:quad], refs[quad:]
    places = partners(quad)
    me = lax.axis_index(AXES[0])
    even = (me & 1) == 0
    start = nothing(load(within_ref))
    for group in range(2 * own_ref.shape[0] - 1):
        same = even if group % 2 == 0 else jnp.logical_not(even)
        own, other = load(own_ref.at[group // 2]), load(other_ref.at[group // 2])
        start = choose(group < me, join(start, choose(same, own, other)), start)
    start = join(start, load(within_ref))
    tops, decays = read_scalars(pieces, scalar_ref, places)
    zero = jnp.zeros_like(tops[0])
    for place in range(quad):
        weights, joined, _ = weights_of([start[2]] + tops[:place], [zero] + decays[:place])
        weights += [zero] * (quad - place)
        for index, weight in enumerate(weights):
            weight_ref[place, index : index + 1, :] = weight
        scalar_ref[0, place : place + 1, :] = joined
    states = [start] + [load(piece) for piece in pieces]
    for place, out_ref in zip(places, out_refs):
        weights = [weight_ref[place, 0:1, :]]
        weights += [weight_ref[place, pl.ds(1 + index, 1), :] for index in places]
        top = scalar_ref[0, pl.ds(place, 1), :]
        store(out_ref, (*weighted_sum(weights, states), top, zero))


CUMUL, ROW_LEVEL, INNER_DEN = range(3)


def inner_kernel(q_ref, k_ref, v_ref, in_ref, fo_ref, num_ref, stat_ref):
    heads, length = in_ref.shape
    key_dim = q_ref.shape[1] // heads
    value_dim = v_ref.shape[1] // heads
    logf = log_forget(fo_ref[...])
    level = in_ref[...] - cumulative_rows(logf)
    cumul = cumulative_columns(logf)
    causal = triangle(length, True)
    for head in range(heads):
        queries = q_ref[:, head * key_dim : (head + 1) * key_dim]
        keys = k_ref[:, head * key_dim : (head + 1) * key_dim]
        values = v_ref[:, head * value_dim : (head + 1) * value_dim]
        scores = dot_last(queries, keys) * (key_dim**-0.5)
        masked = jnp.where(causal, level[head : head + 1, :], -jnp.inf)
        row_level = jnp.max(masked, axis=1, keepdims=True)
        weighted = jnp.exp(masked - row_level) * scores
        stat_ref[head, :, CUMUL : CUMUL + 1] = cumul[:, head : head + 1]
        stat_ref[head, :, ROW_LEVEL : ROW_LEVEL + 1] = row_level
        stat_ref[head, :, INNER_DEN : INNER_DEN + 1] = jnp.sum(weighted, axis=1, keepdims=True)
        num_ref[head] = dot(weighted.astype(jnp.bfloat16), values)


def add_carried(head, q_ref, num_ref, stat_ref, message_ref):
    length, value_dim = num_ref.shape[1:]
    key_dim = q_ref.shape[1] // num_ref.shape[0]
    parts = value_dim // LANES
    scaling = key_dim**-0.5
    query = q_ref[:, pl.ds(pl.multiple_of(head * key_dim, LANES), key_dim)]
    matrix = jnp.concatenate(
        [message_ref[part * key_dim : (part + 1) * key_dim, :] for part in range(parts)], 1
    )
    high, low = split_two(matrix)
    carried = dot(jnp.concatenate([query, query], axis=1), jnp.concatenate([high, low], axis=0))
    stats = stat_ref[head]
    cumul, row_level, inner_den = (stats[:, place : place + 1] for place in range(3))
    top = tail_row(message_ref, TOP)[:, 0:1]
    carried_den = jnp.sum(
        query.astype(jnp.float32) * tail_row(message_ref, VECTOR), axis=1, keepdims=True
    )
    joined = jnp.maximum(row_level, top)
    inner_factor = jnp.exp(row_level - joined)
    outer_factor = jnp.exp(top - joined) * scaling
    denom = inner_factor * inner_den + outer_factor * carried_den
    inverse = 1.0 / jnp.maximum(jnp.abs(denom), jnp.exp(-(cumul + joined)))
    return (inner_factor * inverse) * num_ref[head] + (outer_factor * inverse) * carried


def part_kernel(steps, q_ref, num_ref, stat_ref, *refs):
    places = partners(num_ref.shape[0])
    count = len(steps)
    for step, message_ref, out_ref in zip(steps, refs[:count], refs[count:]):
        head = places[step]
        out_ref[...] = add_carried(head, q_ref, num_ref, stat_ref, message_ref).astype(
            out_ref.dtype
        )


def last_kernel(q_ref, num_ref, stat_ref, message_ref, *refs):
    *done_refs, out_hbm, own_ref, done = refs
    heads, _, value_dim = num_ref.shape
    places = partners(heads)

    def place(step, source):
        columns = pl.ds(pl.multiple_of(places[step] * value_dim, LANES), value_dim)
        copy = pltpu.make_async_copy(source, out_hbm.at[:, columns], done.at[step])
        copy.start()
        return copy

    copies = [place(step, ref) for step, ref in enumerate(done_refs)]
    own_ref[...] = add_carried(places[-1], q_ref, num_ref, stat_ref, message_ref).astype(
        own_ref.dtype
    )
    copies.append(place(heads - 1, own_ref))
    for copy in copies:
        copy.wait()


def swap(array, axis, step):
    count = lax.axis_size(axis)
    return lax.ppermute(array, axis, [(place, place ^ step) for place in range(count)])


def exchange(pieces):
    quad = len(pieces)
    groups, length = (lax.axis_size(axis) for axis in AXES)
    results = [pieces[0]]
    for step in range(1, quad):
        pairs = [
            (group * length + place, group * length + (place ^ distances(quad, group & 1)[step]))
            for group in range(groups)
            for place in range(length)
        ]
        results.append(lax.ppermute(pieces[step], AXES, pairs))
    return results


def on_device(groups, group_length, queries, key_vectors, value_vectors, input_gate, forget_gate):
    heads, length = input_gate.shape
    key_dim = queries.shape[1] // heads
    value_dim = value_vectors.shape[1] // heads
    message = jax.ShapeDtypeStruct(
        (value_dim // LANES * key_dim + TAIL, LANES), jnp.float32
    )
    messages = (message,) * heads
    params = pltpu.CompilerParams(vmem_limit_bytes=48 * 1024 * 1024)
    hbm = pl.BlockSpec(memory_space=pltpu.HBM)
    scalars = pltpu.VMEM((3, heads, LANES), jnp.float32)
    output = jax.ShapeDtypeStruct((length, heads * value_dim), jnp.bfloat16)
    operands = (key_vectors, value_vectors, input_gate, forget_gate)
    own = pl.pallas_call(
        state_kernel,
        out_shape=messages,
        in_specs=[hbm] * len(operands),
        scratch_shapes=[pltpu.VMEM(array.shape, array.dtype) for array in operands]
        + [scalars, pltpu.SemaphoreType.DMA((len(operands),))],
        compiler_params=params,
    )(*(pltpu.with_memory_space_constraint(array, pltpu.HBM) for array in operands))
    pieces = exchange(own)
    inner_num, stats = pl.pallas_call(
        inner_kernel,
        out_shape=(
            jax.ShapeDtypeStruct((heads, length, value_dim), jnp.float32),
            jax.ShapeDtypeStruct((heads, length, 3), jnp.float32),
        ),
        compiler_params=params,
    )(queries, *operands)
    total = pl.pallas_call(
        quad_kernel, out_shape=message, scratch_shapes=[scalars], compiler_params=params
    )(*pieces)
    within = []
    bit = heads
    while bit < group_length:
        total, *within = pl.pallas_call(
            functools.partial(butterfly_kernel, AXES[1], bit),
            out_shape=(message, message),
            compiler_params=params,
        )(total, swap(total, AXES[1], bit), *within)
        bit *= 2
    sums = total
    bit, count = 2, 1
    while bit < groups:
        count *= 2
        sums = pl.pallas_call(
            functools.partial(gather_kernel, AXES[0], bit),
            out_shape=jax.ShapeDtypeStruct((count,) + message.shape, message.dtype),
            compiler_params=params,
        )(sums, swap(sums, AXES[0], bit))
        bit *= 2
    states = pl.pallas_call(
        functools.partial(prefix_kernel, heads),
        out_shape=messages,
        scratch_shapes=[scalars, pltpu.VMEM((heads, 1 + heads, LANES), jnp.float32)],
        compiler_params=params,
    )(sums, swap(sums, AXES[0], 1), *within, *pieces)
    carried = exchange(states)
    column = jax.ShapeDtypeStruct((length, value_dim), output.dtype)
    columns = []
    for steps in [(0, 1)] + [(step,) for step in range(2, heads - 1)]:
        columns += pl.pallas_call(
            functools.partial(part_kernel, steps),
            out_shape=(column,) * len(steps),
            compiler_params=params,
        )(queries, inner_num, stats, *(carried[step] for step in steps))
    return pl.pallas_call(
        last_kernel,
        out_shape=output,
        out_specs=hbm,
        scratch_shapes=[
            pltpu.VMEM(column.shape, column.dtype),
            pltpu.SemaphoreType.DMA((heads,)),
        ],
        compiler_params=params,
    )(queries, inner_num, stats, carried[-1], *columns)


def solution(mesh):
    return jax.shard_map(
        functools.partial(on_device, mesh.shape["grp"], mesh.shape["seq"]),
        mesh=mesh,
        in_specs=(
            P(AXES, None),
            P(AXES, None),
            P(AXES, None),
            P(None, AXES),
            P(None, AXES),
        ),
        out_specs=P(AXES, None),
        check_vma=False,
    )
```

profile of v0, /device:TPU:0, one launch (start us, length us, event | category | flops | bytes accessed | tf_op | source)
XLA Modules:
  0.0 40.2 jit_solution(12812275621344018687)
XLA Ops:
  0.0 1.4 %shard_map.56 = (f32[264,128]{1,0:T(8,128)S(1)}, f32[264,128]{1,0:T(8,128)S(1)}, f32[264,128]{1,0:T(8,128)S(1)}, f32[264,128]{1,0:T(8,128)S(1)}) custom-call(bf16[128,512]{1,0:T(8,128)(2,1)} %k_hbm.1, bf16[128,1024]{1,0:T(8,128)(2,1)} %v_hbm.1, f32[4,128]{1,0:T(4,128)} %in_hbm.1, f32[4,128]{1,0:T(4,128)} %fo_hbm.1), custom_call_target="tpu_custom_call" | custom-call | tf_op jit(solution)/shard_map/pallas_call | solution.py:370
  1.5 3.1 %collective-permute-start = (f32[264,128]{1,0:T(8,128)S(1)}, f32[264,128]{1,0:T(8,128)S(1)}, u32[]{:S(2)}, u32[]{:S(2)}) collective-permute-start(f32[264,128]{1,0:T(8,128)S(1)} %get-tuple-element.22), channel_id=1, source_target_pairs={{0,2},{1,3},{2,0},{3,1},{4,6},{5,7},{6,4},{7,5},{8,9},{9,8},{10,11... | collective-permute-start | bytes 405512 | tf_op jit(solution)/shard_map/ppermute | solution.py:353
  4.5 1.4 %collective-permute-start.1 = (f32[264,128]{1,0:T(8,128)S(1)}, f32[264,128]{1,0:T(8,128)S(1)}, u32[]{:S(2)}, u32[]{:S(2)}) collective-permute-start(f32[264,128]{1,0:T(8,128)S(1)} %get-tuple-element.23), channel_id=1, source_target_pairs={{0,3},{1,2},{2,1},{3,0},{4,7},{5,6},{6,5},{7,4},{8,11},{9,10},{10,... | collective-permute-start | bytes 405512 | tf_op jit(solution)/shard_map/ppermute | solution.py:353
  5.9 0.1 collective-permute-start.2
  6.1 2.6 %collective-permute-done.refs_1_ = f32[264,128]{1,0:T(8,128)S(1)} collective-permute-done((f32[264,128]{1,0:T(8,128)S(1)}, f32[264,128]{1,0:T(8,128)S(1)}, u32[]{:S(2)}, u32[]{:S(2)}) %collective-permute-start) | collective-permute-done | bytes 135200 | tf_op jit(solution)/shard_map/ppermute | solution.py:353
  8.7 4.5 %collective-permute-done.1.refs_2_ = f32[264,128]{1,0:T(8,128)S(1)} collective-permute-done((f32[264,128]{1,0:T(8,128)S(1)}, f32[264,128]{1,0:T(8,128)S(1)}, u32[]{:S(2)}, u32[]{:S(2)}) %collective-permute-start.1) | collective-permute-done | bytes 135200 | tf_op jit(solution)/shard_map/ppermute | solution.py:353
  13.2 0.0 collective-permute-done.2.refs_3_
  13.2 0.1 shard_map.57.refs_0_
  13.3 2.7 %collective-permute-start.3 = (f32[264,128]{1,0:T(8,128)S(1)}, f32[264,128]{1,0:T(8,128)S(1)}, u32[]{:S(2)}, u32[]{:S(2)}) collective-permute-start(f32[264,128]{1,0:T(8,128)S(1)} %shard_map.57.refs_0_), channel_id=1, source_target_pairs={{0,4},{1,5},{2,6},{3,7},{4,0},{5,1},{6,2},{7,3},{8,12},{9,13},{10,... | collective-permute-start | bytes 405512 | tf_op jit(solution)/shard_map/ppermute | solution.py:340
  16.0 5.8 %collective-permute-done.3.refs_1_ = f32[264,128]{1,0:T(8,128)S(1)} collective-permute-done((f32[264,128]{1,0:T(8,128)S(1)}, f32[264,128]{1,0:T(8,128)S(1)}, u32[]{:S(2)}, u32[]{:S(2)}) %collective-permute-start.3) | collective-permute-done | bytes 135200 | tf_op jit(solution)/shard_map/ppermute | solution.py:340
  21.8 0.1 shard_map.58
  21.9 1.6 %collective-permute-start.4 = (f32[264,128]{1,0:T(8,128)S(1)}, f32[264,128]{1,0:T(8,128)S(1)}, u32[]{:S(2)}, u32[]{:S(2)}) collective-permute-start(f32[264,128]{1,0:T(8,128)S(1)} %get-tuple-element.25.own_ref), channel_id=1, source_target_pairs={{0,16},{8,24},{16,0},{24,8},{1,17},{9,25},{17,1},{25,9},{2,18},{10... | collective-permute-start | bytes 405512 | tf_op jit(solution)/shard_map/ppermute | solution.py:340
  23.5 3.5 %collective-permute-done.4.other_ref = f32[264,128]{1,0:T(8,128)S(1)} collective-permute-done((f32[264,128]{1,0:T(8,128)S(1)}, f32[264,128]{1,0:T(8,128)S(1)}, u32[]{:S(2)}, u32[]{:S(2)}) %collective-permute-start.4) | collective-permute-done | bytes 135200 | tf_op jit(solution)/shard_map/ppermute | solution.py:340
  27.0 0.1 collective-permute-start.5
  27.1 1.5 %collective-permute-done.5.other_ref = f32[2,264,128]{2,1,0:T(8,128)S(1)} collective-permute-done((f32[2,264,128]{2,1,0:T(8,128)S(1)}, f32[2,264,128]{2,1,0:T(8,128)S(1)}, u32[]{:S(2)}, u32[]{:S(2)}) %collective-permute-start.5) | collective-permute-done | bytes 270368 | tf_op jit(solution)/shard_map/ppermute | solution.py:340
  28.6 0.0 copy-start
  28.6 0.0 copy-start.1
  28.6 0.0 copy-start.2
  28.6 0.4 shard_map.60
  29.0 0.0 copy-start.4
  29.0 0.0 copy-start.3
  29.0 2.1 %collective-permute-start.8 = (f32[264,128]{1,0:T(8,128)S(1)}, f32[264,128]{1,0:T(8,128)S(1)}, u32[]{:S(2)}, u32[]{:S(2)}) collective-permute-start(f32[264,128]{1,0:T(8,128)S(1)} %get-tuple-element.32), channel_id=1, source_target_pairs={{0,3},{1,2},{2,1},{3,0},{4,7},{5,6},{6,5},{7,4},{8,11},{9,10},{10,... | collective-permute-start | bytes 405512 | tf_op jit(solution)/shard_map/ppermute | solution.py:353
  31.2 0.9 %collective-permute-start.7 = (f32[264,128]{1,0:T(8,128)S(1)}, f32[264,128]{1,0:T(8,128)S(1)}, u32[]{:S(2)}, u32[]{:S(2)}) collective-permute-start(f32[264,128]{1,0:T(8,128)S(1)} %get-tuple-element.29), channel_id=1, source_target_pairs={{0,2},{1,3},{2,0},{3,1},{4,6},{5,7},{6,4},{7,5},{8,9},{9,8},{10,11... | collective-permute-start | bytes 405512 | tf_op jit(solution)/shard_map/ppermute | solution.py:353
  32.0 0.5 %collective-permute-start.6 = (f32[264,128]{1,0:T(8,128)S(1)}, f32[264,128]{1,0:T(8,128)S(1)}, u32[]{:S(2)}, u32[]{:S(2)}) collective-permute-start(f32[264,128]{1,0:T(8,128)S(1)} %get-tuple-element.27), channel_id=1, source_target_pairs={{0,1},{1,0},{2,3},{3,2},{4,5},{5,4},{6,7},{7,6},{8,10},{9,11},{10,... | collective-permute-start | bytes 405512 | tf_op jit(solution)/shard_map/ppermute | solution.py:353
  32.6 0.0 copy-done
  32.6 0.0 copy-done.1
  32.6 0.0 copy-done.2
  32.6 0.0 copy-done.4
  32.6 0.0 copy-done.3
  32.6 0.9 %shard_map.55 = (f32[4,128,256]{2,1,0:T(8,128)S(1)}, f32[4,128,3]{2,1,0:T(8,128)S(1)}) custom-call(bf16[128,512]{1,0:T(8,128)(2,1)S(1)} %copy-done, bf16[128,512]{1,0:T(8,128)(2,1)S(1)} %copy-done.2, bf16[128,1024]{1,0:T(8,128)(2,1)S(1)} %copy-done.1, f32[4,128]{1,0:T(4,128)S(1)} %copy-done.3, f32[4,128]{1,0:T(4,128)S(1)} %copy-done.4), custom_call_target="tpu_custom_call" | custom-call | tf_op jit(solution)/shard_map/pallas_call | solution.py:379
  33.5 2.9 %collective-permute-done.8.refs_0_ = f32[264,128]{1,0:T(8,128)S(1)} collective-permute-done((f32[264,128]{1,0:T(8,128)S(1)}, f32[264,128]{1,0:T(8,128)S(1)}, u32[]{:S(2)}, u32[]{:S(2)}) %collective-permute-start.8) | collective-permute-done | bytes 135200 | tf_op jit(solution)/shard_map/ppermute | solution.py:353
  36.4 0.4 %shard_map.62.refs_2_ = bf16[128,256]{1,0:T(8,128)(2,1)S(1)} custom-call(bf16[128,512]{1,0:T(8,128)(2,1)S(1)} %copy-done, f32[4,128,256]{2,1,0:T(8,128)S(1)} %get-tuple-element.19.num_ref, f32[4,128,3]{2,1,0:T(8,128)S(1)} %get-tuple-element.20.stat_ref, f32[264,128]{1,0:T(8,128)S(1)} %collective-permute-done.8.refs_0_), custom_call_target="tpu_custom_call" | custom-call | tf_op jit(solution)/shard_map/pallas_call | solution.py:419
  36.8 1.8 %collective-permute-done.7.refs_1_ = f32[264,128]{1,0:T(8,128)S(1)} collective-permute-done((f32[264,128]{1,0:T(8,128)S(1)}, f32[264,128]{1,0:T(8,128)S(1)}, u32[]{:S(2)}, u32[]{:S(2)}) %collective-permute-start.7) | collective-permute-done | bytes 135200 | tf_op jit(solution)/shard_map/ppermute | solution.py:353
  38.6 0.6 %shard_map.61 = (bf16[128,256]{1,0:T(8,128)(2,1)S(1)}, bf16[128,256]{1,0:T(8,128)(2,1)S(1)}) custom-call(bf16[128,512]{1,0:T(8,128)(2,1)S(1)} %copy-done, f32[4,128,256]{2,1,0:T(8,128)S(1)} %get-tuple-element.19.num_ref, f32[4,128,3]{2,1,0:T(8,128)S(1)} %get-tuple-element.20.stat_ref, f32[264,128]{1,0:T(8,128)S(1)} %get-tuple-element.28.refs_0_, ...), custom_call_target="tpu_custom_call" | custom-call | tf_op jit(solution)/shard_map/pallas_call | solution.py:419
  39.2 0.0 collective-permute-done.6.message_ref
  39.2 1.1 %shard_map.63 = bf16[128,1024]{1,0:T(8,128)(2,1)} custom-call(bf16[128,512]{1,0:T(8,128)(2,1)S(1)} %copy-done, f32[4,128,256]{2,1,0:T(8,128)S(1)} %get-tuple-element.19.num_ref, f32[4,128,3]{2,1,0:T(8,128)S(1)} %get-tuple-element.20.stat_ref, f32[264,128]{1,0:T(8,128)S(1)} %collective-permute-done.6.message_ref, ...), custom_call_target="tpu_custom_call" | custom-call | tf_op jit(solution)/shard_map/pallas_call | solution.py:424
  (1 shorter events, 0.0 us)
Async XLA Ops:
  1.5 7.2 %collective-permute-start = (f32[264,128]{1,0:T(8,128)S(1)}, f32[264,128]{1,0:T(8,128)S(1)}, u32[]{:S(2)}, u32[]{:S(2)}) collective-permute-start(f32[264,128]{1,0:T(8,128)S(1)} %get-tuple-element.22), channel_id=1, source_target_pairs={{0,2},{1,3},{2,0},{3,1},{4,6},{5,7},{6,4},{7,5},{8,9},{9,8},{10,11... | collective-permute-start | bytes 405512 | tf_op jit(solution)/shard_map/ppermute | solution.py:353
  4.5 8.7 %collective-permute-start.1 = (f32[264,128]{1,0:T(8,128)S(1)}, f32[264,128]{1,0:T(8,128)S(1)}, u32[]{:S(2)}, u32[]{:S(2)}) collective-permute-start(f32[264,128]{1,0:T(8,128)S(1)} %get-tuple-element.23), channel_id=1, source_target_pairs={{0,3},{1,2},{2,1},{3,0},{4,7},{5,6},{6,5},{7,4},{8,11},{9,10},{10,... | collective-permute-start | bytes 405512 | tf_op jit(solution)/shard_map/ppermute | solution.py:353
  5.9 7.3 %collective-permute-start.2 = (f32[264,128]{1,0:T(8,128)S(1)}, f32[264,128]{1,0:T(8,128)S(1)}, u32[]{:S(2)}, u32[]{:S(2)}) collective-permute-start(f32[264,128]{1,0:T(8,128)S(1)} %get-tuple-element.24), channel_id=1, source_target_pairs={{0,1},{1,0},{2,3},{3,2},{4,5},{5,4},{6,7},{7,6},{8,10},{9,11},{10,... | collective-permute-start | bytes 405512 | tf_op jit(solution)/shard_map/ppermute | solution.py:353
  13.3 8.5 %collective-permute-start.3 = (f32[264,128]{1,0:T(8,128)S(1)}, f32[264,128]{1,0:T(8,128)S(1)}, u32[]{:S(2)}, u32[]{:S(2)}) collective-permute-start(f32[264,128]{1,0:T(8,128)S(1)} %shard_map.57.refs_0_), channel_id=1, source_target_pairs={{0,4},{1,5},{2,6},{3,7},{4,0},{5,1},{6,2},{7,3},{8,12},{9,13},{10,... | collective-permute-start | bytes 405512 | tf_op jit(solution)/shard_map/ppermute | solution.py:340
  21.9 5.1 %collective-permute-start.4 = (f32[264,128]{1,0:T(8,128)S(1)}, f32[264,128]{1,0:T(8,128)S(1)}, u32[]{:S(2)}, u32[]{:S(2)}) collective-permute-start(f32[264,128]{1,0:T(8,128)S(1)} %get-tuple-element.25.own_ref), channel_id=1, source_target_pairs={{0,16},{8,24},{16,0},{24,8},{1,17},{9,25},{17,1},{25,9},{2,18},{10... | collective-permute-start | bytes 405512 | tf_op jit(solution)/shard_map/ppermute | solution.py:340
  27.0 1.6 %collective-permute-start.5 = (f32[2,264,128]{2,1,0:T(8,128)S(1)}, f32[2,264,128]{2,1,0:T(8,128)S(1)}, u32[]{:S(2)}, u32[]{:S(2)}) collective-permute-start(f32[2,264,128]{2,1,0:T(8,128)S(1)} %shard_map.59.own_ref), channel_id=1, source_target_pairs={{0,8},{8,0},{16,24},{24,16},{1,9},{9,1},{17,25},{25,17},{2,10},{10... | collective-permute-start | bytes 811016 | tf_op jit(solution)/shard_map/ppermute | solution.py:340
  28.6 4.0 %copy-start = (bf16[128,512]{1,0:T(8,128)(2,1)S(1)}, bf16[128,512]{1,0:T(8,128)(2,1)}, u32[]{:S(2)}) copy-start(bf16[128,512]{1,0:T(8,128)(2,1)} %q_ref.7) | copy-start | bytes 393220
  28.6 4.0 %copy-start.1 = (bf16[128,1024]{1,0:T(8,128)(2,1)S(1)}, bf16[128,1024]{1,0:T(8,128)(2,1)}, u32[]{:S(2)}) copy-start(bf16[128,1024]{1,0:T(8,128)(2,1)} %v_hbm.1) | copy-start | bytes 786436
  28.6 4.0 %copy-start.2 = (bf16[128,512]{1,0:T(8,128)(2,1)S(1)}, bf16[128,512]{1,0:T(8,128)(2,1)}, u32[]{:S(2)}) copy-start(bf16[128,512]{1,0:T(8,128)(2,1)} %k_hbm.1) | copy-start | bytes 393220
  29.0 3.6 %copy-start.4 = (f32[4,128]{1,0:T(4,128)S(1)}, f32[4,128]{1,0:T(4,128)}, u32[]{:S(2)}) copy-start(f32[4,128]{1,0:T(4,128)} %fo_hbm.1) | copy-start | bytes 6148
  29.0 3.6 %copy-start.3 = (f32[4,128]{1,0:T(4,128)S(1)}, f32[4,128]{1,0:T(4,128)}, u32[]{:S(2)}) copy-start(f32[4,128]{1,0:T(4,128)} %in_hbm.1) | copy-start | bytes 6148
  29.0 7.4 %collective-permute-start.8 = (f32[264,128]{1,0:T(8,128)S(1)}, f32[264,128]{1,0:T(8,128)S(1)}, u32[]{:S(2)}, u32[]{:S(2)}) collective-permute-start(f32[264,128]{1,0:T(8,128)S(1)} %get-tuple-element.32), channel_id=1, source_target_pairs={{0,3},{1,2},{2,1},{3,0},{4,7},{5,6},{6,5},{7,4},{8,11},{9,10},{10,... | collective-permute-start | bytes 405512 | tf_op jit(solution)/shard_map/ppermute | solution.py:353
  31.2 7.4 %collective-permute-start.7 = (f32[264,128]{1,0:T(8,128)S(1)}, f32[264,128]{1,0:T(8,128)S(1)}, u32[]{:S(2)}, u32[]{:S(2)}) collective-permute-start(f32[264,128]{1,0:T(8,128)S(1)} %get-tuple-element.29), channel_id=1, source_target_pairs={{0,2},{1,3},{2,0},{3,1},{4,6},{5,7},{6,4},{7,5},{8,9},{9,8},{10,11... | collective-permute-start | bytes 405512 | tf_op jit(solution)/shard_map/ppermute | solution.py:353
  32.0 7.1 %collective-permute-start.6 = (f32[264,128]{1,0:T(8,128)S(1)}, f32[264,128]{1,0:T(8,128)S(1)}, u32[]{:S(2)}, u32[]{:S(2)}) collective-permute-start(f32[264,128]{1,0:T(8,128)S(1)} %get-tuple-element.27), channel_id=1, source_target_pairs={{0,1},{1,0},{2,3},{3,2},{4,5},{5,4},{6,7},{7,6},{8,10},{9,11},{10,... | collective-permute-start | bytes 405512 | tf_op jit(solution)/shard_map/ppermute | solution.py:353
where the time goes:
time: 40.4 us; the launch traced here: 40.2 us
  waiting for transfers between devices  22.7 us (56%)
  starting transfers between devices  12.5 us (31%)
  Pallas kernels  4.93 us (12%)
    ppermute x6, waiting for transfers between devices, exchange(): results.append(lax.ppermute(pieces[step], AXES, pairs))  11.8 us
    ppermute x3, waiting for transfers between devices, swap(): lax.ppermute(array, axis, [(place, place ^ step) for place in range(count)])  10.8 us
    ppermute x6, starting transfers between devices, exchange(): results.append(lax.ppermute(pieces[step], AXES, pairs))  8.19 us
    ppermute x3, starting transfers between devices, swap(): lax.ppermute(array, axis, [(place, place ^ step) for place in range(count)])  4.33 us
    pallas_call x1, Pallas kernels, on_device(): pl.pallas_call(state_kernel, out_shape=messages, in_specs=[hbm] * len(ope...  1.44 us
    pallas_call x1, Pallas kernels, on_device(): pl.pallas_call(last_kernel, out_shape=output, out_specs=hbm, scratch_shap...  1.08 us
    pallas_call x2, Pallas kernels, on_device(): pl.pallas_call(functools.partial(part_kernel, steps), out_shape=(column,)...  0.99 us
    pallas_call x1, Pallas kernels, on_device(): pl.pallas_call(inner_kernel, out_shape=(jax.ShapeDtypeStruct((heads, leng...  0.88 us
  transfers between devices with their start and end apart: 9, of which 7 were waited for; matrix products, arithmetic and copies ran while one was open for 0% of the time, Pallas kernels for 5%

commit v1 on v0

--- a/solution.py
+++ b/solution.py
@@ -64,20 +64,8 @@
     return lax.rem(lax.axis_index(AXES[1]), quad)
 
 
-def distances(quad, side):
-    order = [0, 1, quad - 1, *range(2, quad - 1)]
-    bits = quad.bit_length() - 1
-    if side:
-        return order
-    return [sum(((step >> bit) & 1) << (bits - 1 - bit) for bit in range(bits)) for step in order]
-
-
 def partners(quad):
-    even = (lax.axis_index(AXES[0]) & 1) == 0
-    return [
-        member(quad) ^ jnp.where(even, one, other)
-        for one, other in zip(distances(quad, 0), distances(quad, 1))
-    ]
+    return [member(quad) ^ step for step in range(quad)]
 
 
 def tail_rows(vector, top, decay):
@@ -341,17 +329,7 @@
 
 
 def exchange(pieces):
-    quad = len(pieces)
-    groups, length = (lax.axis_size(axis) for axis in AXES)
-    results = [pieces[0]]
-    for step in range(1, quad):
-        pairs = [
-            (group * length + place, group * length + (place ^ distances(quad, group & 1)[step]))
-            for group in range(groups)
-            for place in range(length)
-        ]
-        results.append(lax.ppermute(pieces[step], AXES, pairs))
-    return results
+    return [pieces[0]] + [swap(pieces[step], AXES[1], step) for step in range(1, len(pieces))]
 
 
 def on_device(groups, group_length, queries, key_vectors, value_vectors, input_gate, forget_gate):

time: 40.4 us -> 38.1 us (0.943)
  waiting for transfers between devices: 22.7 us -> 20.3 us
    ppermute x6 -> x0, waiting for transfers between devices: 11.8 us -> none  [exchange(): results.append(lax.ppermute(pieces[step], AXES, pairs))]
    ppermute x3 -> x9, waiting for transfers between devices: 10.8 us -> 20.3 us  [swap(): lax.ppermute(array, axis, [(place, place ^ step) for place in range(count)])]
    ppermute x3 -> x9, starting transfers between devices: 4.33 us -> 12.6 us  [swap(): lax.ppermute(array, axis, [(place, place ^ step) for place in range(count)])]
    ppermute x6 -> x0, starting transfers between devices: 8.19 us -> none  [exchange(): results.append(lax.ppermute(pieces[step], AXES, pairs))]
  transfers between devices with their start and end apart: 9 -> 9, of which waited for: 7 -> 8; matrix products, arithmetic and copies ran while one was open for 0% -> 0% of each run, Pallas kernels for 5% -> 5%
where the time goes in v1:
time: 38.1 us; the launch traced here: 38 us
  waiting for transfers between devices  20.3 us (53%)
  starting transfers between devices  12.6 us (33%)
  Pallas kernels  4.95 us (13%)
    ppermute x9, waiting for transfers between devices, swap(): lax.ppermute(array, axis, [(place, place ^ step) for place in range(count)])  20.3 us
    ppermute x9, starting transfers between devices, swap(): lax.ppermute(array, axis, [(place, place ^ step) for place in range(count)])  12.6 us
    pallas_call x1, Pallas kernels, on_device(): pl.pallas_call(state_kernel, out_shape=messages, in_specs=[hbm] * len(ope...  1.44 us
    pallas_call x1, Pallas kernels, on_device(): pl.pallas_call(last_kernel, out_shape=output, out_specs=hbm, scratch_shap...  1.08 us
    pallas_call x2, Pallas kernels, on_device(): pl.pallas_call(functools.partial(part_kernel, steps), out_shape=(column,)...  1.01 us
    pallas_call x1, Pallas kernels, on_device(): pl.pallas_call(inner_kernel, out_shape=(jax.ShapeDtypeStruct((heads, leng...  0.88 us
  transfers between devices with their start and end apart: 9, of which 8 were waited for; matrix products, arithmetic and copies ran while one was open for 0% of the time, Pallas kernels for 5%

profile of v1, /device:TPU:0, one launch (start us, length us, event | category | flops | bytes accessed | tf_op | source)
XLA Modules:
  0.0 38.0 jit_solution(1283304910743104944)
XLA Ops:
  0.0 1.4 %shard_map.56 = (f32[264,128]{1,0:T(8,128)S(1)}, f32[264,128]{1,0:T(8,128)S(1)}, f32[264,128]{1,0:T(8,128)S(1)}, f32[264,128]{1,0:T(8,128)S(1)}) custom-call(bf16[128,512]{1,0:T(8,128)(2,1)} %k_hbm.1, bf16[128,1024]{1,0:T(8,128)(2,1)} %v_hbm.1, f32[4,128]{1,0:T(4,128)} %in_hbm.1, f32[4,128]{1,0:T(4,128)} %fo_hbm.1), custom_call_target="tpu_custom_call" | custom-call | tf_op jit(solution)/shard_map/pallas_call | solution.py:348
  1.5 3.0 %collective-permute-start = (f32[264,128]{1,0:T(8,128)S(1)}, f32[264,128]{1,0:T(8,128)S(1)}, u32[]{:S(2)}, u32[]{:S(2)}) collective-permute-start(f32[264,128]{1,0:T(8,128)S(1)} %get-tuple-element.22), channel_id=1, source_target_pairs={{0,1},{1,0},{2,3},{3,2},{4,5},{5,4},{6,7},{7,6},{8,9},{9,8},{10,11... | collective-permute-start | bytes 405512 | tf_op jit(solution)/shard_map/ppermute | solution.py:328
  4.5 1.6 %collective-permute-start.1 = (f32[264,128]{1,0:T(8,128)S(1)}, f32[264,128]{1,0:T(8,128)S(1)}, u32[]{:S(2)}, u32[]{:S(2)}) collective-permute-start(f32[264,128]{1,0:T(8,128)S(1)} %get-tuple-element.23), channel_id=1, source_target_pairs={{0,2},{1,3},{2,0},{3,1},{4,6},{5,7},{6,4},{7,5},{8,10},{9,11},{10,... | collective-permute-start | bytes 405512 | tf_op jit(solution)/shard_map/ppermute | solution.py:328
  6.1 0.0 collective-permute-start.2
  6.1 2.0 %collective-permute-done.refs_1_ = f32[264,128]{1,0:T(8,128)S(1)} collective-permute-done((f32[264,128]{1,0:T(8,128)S(1)}, f32[264,128]{1,0:T(8,128)S(1)}, u32[]{:S(2)}, u32[]{:S(2)}) %collective-permute-start) | collective-permute-done | bytes 135200 | tf_op jit(solution)/shard_map/ppermute | solution.py:328
  8.1 2.9 %collective-permute-done.1.refs_2_ = f32[264,128]{1,0:T(8,128)S(1)} collective-permute-done((f32[264,128]{1,0:T(8,128)S(1)}, f32[264,128]{1,0:T(8,128)S(1)}, u32[]{:S(2)}, u32[]{:S(2)}) %collective-permute-start.1) | collective-permute-done | bytes 135200 | tf_op jit(solution)/shard_map/ppermute | solution.py:328
  11.0 1.2 %collective-permute-done.2.refs_3_ = f32[264,128]{1,0:T(8,128)S(1)} collective-permute-done((f32[264,128]{1,0:T(8,128)S(1)}, f32[264,128]{1,0:T(8,128)S(1)}, u32[]{:S(2)}, u32[]{:S(2)}) %collective-permute-start.2) | collective-permute-done | bytes 135200 | tf_op jit(solution)/shard_map/ppermute | solution.py:328
  12.2 0.1 shard_map.57.refs_0_
  12.3 2.8 %collective-permute-start.3 = (f32[264,128]{1,0:T(8,128)S(1)}, f32[264,128]{1,0:T(8,128)S(1)}, u32[]{:S(2)}, u32[]{:S(2)}) collective-permute-start(f32[264,128]{1,0:T(8,128)S(1)} %shard_map.57.refs_0_), channel_id=1, source_target_pairs={{0,4},{1,5},{2,6},{3,7},{4,0},{5,1},{6,2},{7,3},{8,12},{9,13},{10,... | collective-permute-start | bytes 405512 | tf_op jit(solution)/shard_map/ppermute | solution.py:328
  15.1 5.6 %collective-permute-done.3.refs_1_ = f32[264,128]{1,0:T(8,128)S(1)} collective-permute-done((f32[264,128]{1,0:T(8,128)S(1)}, f32[264,128]{1,0:T(8,128)S(1)}, u32[]{:S(2)}, u32[]{:S(2)}) %collective-permute-start.3) | collective-permute-done | bytes 135200 | tf_op jit(solution)/shard_map/ppermute | solution.py:328
  20.7 0.1 shard_map.58
  20.8 1.6 %collective-permute-start.4 = (f32[264,128]{1,0:T(8,128)S(1)}, f32[264,128]{1,0:T(8,128)S(1)}, u32[]{:S(2)}, u32[]{:S(2)}) collective-permute-start(f32[264,128]{1,0:T(8,128)S(1)} %get-tuple-element.25.own_ref), channel_id=1, source_target_pairs={{0,16},{8,24},{16,0},{24,8},{1,17},{9,25},{17,1},{25,9},{2,18},{10... | collective-permute-start | bytes 405512 | tf_op jit(solution)/shard_map/ppermute | solution.py:328
  22.4 3.5 %collective-permute-done.4.other_ref = f32[264,128]{1,0:T(8,128)S(1)} collective-permute-done((f32[264,128]{1,0:T(8,128)S(1)}, f32[264,128]{1,0:T(8,128)S(1)}, u32[]{:S(2)}, u32[]{:S(2)}) %collective-permute-start.4) | collective-permute-done | bytes 135200 | tf_op jit(solution)/shard_map/ppermute | solution.py:328
  25.9 0.1 collective-permute-start.5
  26.0 1.5 %collective-permute-done.5.other_ref = f32[2,264,128]{2,1,0:T(8,128)S(1)} collective-permute-done((f32[2,264,128]{2,1,0:T(8,128)S(1)}, f32[2,264,128]{2,1,0:T(8,128)S(1)}, u32[]{:S(2)}, u32[]{:S(2)}) %collective-permute-start.5) | collective-permute-done | bytes 270368 | tf_op jit(solution)/shard_map/ppermute | solution.py:328
  27.5 0.0 copy-start
  27.5 0.0 copy-start.1
  27.5 0.0 copy-start.2
  27.5 0.4 shard_map.60
  27.9 0.0 copy-start.4
  27.9 0.0 copy-start.3
  27.9 0.3 collective-permute-start.8
  28.2 1.4 %collective-permute-start.7 = (f32[264,128]{1,0:T(8,128)S(1)}, f32[264,128]{1,0:T(8,128)S(1)}, u32[]{:S(2)}, u32[]{:S(2)}) collective-permute-start(f32[264,128]{1,0:T(8,128)S(1)} %get-tuple-element.29), channel_id=1, source_target_pairs={{0,1},{1,0},{2,3},{3,2},{4,5},{5,4},{6,7},{7,6},{8,9},{9,8},{10,11... | collective-permute-start | bytes 405512 | tf_op jit(solution)/shard_map/ppermute | solution.py:328
  29.6 1.9 %collective-permute-start.6 = (f32[264,128]{1,0:T(8,128)S(1)}, f32[264,128]{1,0:T(8,128)S(1)}, u32[]{:S(2)}, u32[]{:S(2)}) collective-permute-start(f32[264,128]{1,0:T(8,128)S(1)} %get-tuple-element.27), channel_id=1, source_target_pairs={{0,3},{1,2},{2,1},{3,0},{4,7},{5,6},{6,5},{7,4},{8,11},{9,10},{10,... | collective-permute-start | bytes 405512 | tf_op jit(solution)/shard_map/ppermute | solution.py:328
  31.5 0.0 copy-done
  31.5 0.0 copy-done.1
  31.5 0.0 copy-done.2
  31.5 0.0 copy-done.4
  31.5 0.0 copy-done.3
  31.5 0.9 %shard_map.55 = (f32[4,128,256]{2,1,0:T(8,128)S(1)}, f32[4,128,3]{2,1,0:T(8,128)S(1)}) custom-call(bf16[128,512]{1,0:T(8,128)(2,1)S(1)} %copy-done, bf16[128,512]{1,0:T(8,128)(2,1)S(1)} %copy-done.2, bf16[128,1024]{1,0:T(8,128)(2,1)S(1)} %copy-done.1, f32[4,128]{1,0:T(4,128)S(1)} %copy-done.3, f32[4,128]{1,0:T(4,128)S(1)} %copy-done.4), custom_call_target="tpu_custom_call" | custom-call | tf_op jit(solution)/shard_map/pallas_call | solution.py:357
  32.4 2.0 %collective-permute-done.8.refs_0_ = f32[264,128]{1,0:T(8,128)S(1)} collective-permute-done((f32[264,128]{1,0:T(8,128)S(1)}, f32[264,128]{1,0:T(8,128)S(1)}, u32[]{:S(2)}, u32[]{:S(2)}) %collective-permute-start.8) | collective-permute-done | bytes 135200 | tf_op jit(solution)/shard_map/ppermute | solution.py:328
  34.4 0.4 %shard_map.62.refs_2_ = bf16[128,256]{1,0:T(8,128)(2,1)S(1)} custom-call(bf16[128,512]{1,0:T(8,128)(2,1)S(1)} %copy-done, f32[4,128,256]{2,1,0:T(8,128)S(1)} %get-tuple-element.19.num_ref, f32[4,128,3]{2,1,0:T(8,128)S(1)} %get-tuple-element.20.stat_ref, f32[264,128]{1,0:T(8,128)S(1)} %collective-permute-done.8.refs_0_), custom_call_target="tpu_custom_call" | custom-call | tf_op jit(solution)/shard_map/pallas_call | solution.py:397
  34.8 0.0 collective-permute-done.7.refs_1_
  34.9 0.6 %shard_map.61 = (bf16[128,256]{1,0:T(8,128)(2,1)S(1)}, bf16[128,256]{1,0:T(8,128)(2,1)S(1)}) custom-call(bf16[128,512]{1,0:T(8,128)(2,1)S(1)} %copy-done, f32[4,128,256]{2,1,0:T(8,128)S(1)} %get-tuple-element.19.num_ref, f32[4,128,3]{2,1,0:T(8,128)S(1)} %get-tuple-element.20.stat_ref, f32[264,128]{1,0:T(8,128)S(1)} %get-tuple-element.28.refs_0_, ...), custom_call_target="tpu_custom_call" | custom-call | tf_op jit(solution)/shard_map/pallas_call | solution.py:397
  35.5 1.4 %collective-permute-done.6.message_ref = f32[264,128]{1,0:T(8,128)S(1)} collective-permute-done((f32[264,128]{1,0:T(8,128)S(1)}, f32[264,128]{1,0:T(8,128)S(1)}, u32[]{:S(2)}, u32[]{:S(2)}) %collective-permute-start.6) | collective-permute-done | bytes 135200 | tf_op jit(solution)/shard_map/ppermute | solution.py:328
  36.9 1.1 %shard_map.63 = bf16[128,1024]{1,0:T(8,128)(2,1)} custom-call(bf16[128,512]{1,0:T(8,128)(2,1)S(1)} %copy-done, f32[4,128,256]{2,1,0:T(8,128)S(1)} %get-tuple-element.19.num_ref, f32[4,128,3]{2,1,0:T(8,128)S(1)} %get-tuple-element.20.stat_ref, f32[264,128]{1,0:T(8,128)S(1)} %collective-permute-done.6.message_ref, ...), custom_call_target="tpu_custom_call" | custom-call | tf_op jit(solution)/shard_map/pallas_call | solution.py:402
  (1 shorter events, 0.0 us)
Async XLA Ops:
  1.5 6.6 %collective-permute-start = (f32[264,128]{1,0:T(8,128)S(1)}, f32[264,128]{1,0:T(8,128)S(1)}, u32[]{:S(2)}, u32[]{:S(2)}) collective-permute-start(f32[264,128]{1,0:T(8,128)S(1)} %get-tuple-element.22), channel_id=1, source_target_pairs={{0,1},{1,0},{2,3},{3,2},{4,5},{5,4},{6,7},{7,6},{8,9},{9,8},{10,11... | collective-permute-start | bytes 405512 | tf_op jit(solution)/shard_map/ppermute | solution.py:328
  4.5 6.5 %collective-permute-start.1 = (f32[264,128]{1,0:T(8,128)S(1)}, f32[264,128]{1,0:T(8,128)S(1)}, u32[]{:S(2)}, u32[]{:S(2)}) collective-permute-start(f32[264,128]{1,0:T(8,128)S(1)} %get-tuple-element.23), channel_id=1, source_target_pairs={{0,2},{1,3},{2,0},{3,1},{4,6},{5,7},{6,4},{7,5},{8,10},{9,11},{10,... | collective-permute-start | bytes 405512 | tf_op jit(solution)/shard_map/ppermute | solution.py:328
  6.1 6.2 %collective-permute-start.2 = (f32[264,128]{1,0:T(8,128)S(1)}, f32[264,128]{1,0:T(8,128)S(1)}, u32[]{:S(2)}, u32[]{:S(2)}) collective-permute-start(f32[264,128]{1,0:T(8,128)S(1)} %get-tuple-element.24), channel_id=1, source_target_pairs={{0,3},{1,2},{2,1},{3,0},{4,7},{5,6},{6,5},{7,4},{8,11},{9,10},{10,... | collective-permute-start | bytes 405512 | tf_op jit(solution)/shard_map/ppermute | solution.py:328
  12.3 8.4 %collective-permute-start.3 = (f32[264,128]{1,0:T(8,128)S(1)}, f32[264,128]{1,0:T(8,128)S(1)}, u32[]{:S(2)}, u32[]{:S(2)}) collective-permute-start(f32[264,128]{1,0:T(8,128)S(1)} %shard_map.57.refs_0_), channel_id=1, source_target_pairs={{0,4},{1,5},{2,6},{3,7},{4,0},{5,1},{6,2},{7,3},{8,12},{9,13},{10,... | collective-permute-start | bytes 405512 | tf_op jit(solution)/shard_map/ppermute | solution.py:328
  20.8 5.1 %collective-permute-start.4 = (f32[264,128]{1,0:T(8,128)S(1)}, f32[264,128]{1,0:T(8,128)S(1)}, u32[]{:S(2)}, u32[]{:S(2)}) collective-permute-start(f32[264,128]{1,0:T(8,128)S(1)} %get-tuple-element.25.own_ref), channel_id=1, source_target_pairs={{0,16},{8,24},{16,0},{24,8},{1,17},{9,25},{17,1},{25,9},{2,18},{10... | collective-permute-start | bytes 405512 | tf_op jit(solution)/shard_map/ppermute | solution.py:328
  25.9 1.6 %collective-permute-start.5 = (f32[2,264,128]{2,1,0:T(8,128)S(1)}, f32[2,264,128]{2,1,0:T(8,128)S(1)}, u32[]{:S(2)}, u32[]{:S(2)}) collective-permute-start(f32[2,264,128]{2,1,0:T(8,128)S(1)} %shard_map.59.own_ref), channel_id=1, source_target_pairs={{0,8},{8,0},{16,24},{24,16},{1,9},{9,1},{17,25},{25,17},{2,10},{10... | collective-permute-start | bytes 811016 | tf_op jit(solution)/shard_map/ppermute | solution.py:328
  27.5 4.0 %copy-start = (bf16[128,512]{1,0:T(8,128)(2,1)S(1)}, bf16[128,512]{1,0:T(8,128)(2,1)}, u32[]{:S(2)}) copy-start(bf16[128,512]{1,0:T(8,128)(2,1)} %q_ref.7) | copy-start | bytes 393220
  27.5 4.0 %copy-start.1 = (bf16[128,1024]{1,0:T(8,128)(2,1)S(1)}, bf16[128,1024]{1,0:T(8,128)(2,1)}, u32[]{:S(2)}) copy-start(bf16[128,1024]{1,0:T(8,128)(2,1)} %v_hbm.1) | copy-start | bytes 786436
  27.5 4.0 %copy-start.2 = (bf16[128,512]{1,0:T(8,128)(2,1)S(1)}, bf16[128,512]{1,0:T(8,128)(2,1)}, u32[]{:S(2)}) copy-start(bf16[128,512]{1,0:T(8,128)(2,1)} %k_hbm.1) | copy-start | bytes 393220
  27.9 3.6 %copy-start.4 = (f32[4,128]{1,0:T(4,128)S(1)}, f32[4,128]{1,0:T(4,128)}, u32[]{:S(2)}) copy-start(f32[4,128]{1,0:T(4,128)} %fo_hbm.1) | copy-start | bytes 6148
  27.9 3.6 %copy-start.3 = (f32[4,128]{1,0:T(4,128)S(1)}, f32[4,128]{1,0:T(4,128)}, u32[]{:S(2)}) copy-start(f32[4,128]{1,0:T(4,128)} %in_hbm.1) | copy-start | bytes 6148
  27.9 6.5 %collective-permute-start.8 = (f32[264,128]{1,0:T(8,128)S(1)}, f32[264,128]{1,0:T(8,128)S(1)}, u32[]{:S(2)}, u32[]{:S(2)}) collective-permute-start(f32[264,128]{1,0:T(8,128)S(1)} %get-tuple-element.32), channel_id=1, source_target_pairs={{0,2},{1,3},{2,0},{3,1},{4,6},{5,7},{6,4},{7,5},{8,10},{9,11},{10,... | collective-permute-start | bytes 405512 | tf_op jit(solution)/shard_map/ppermute | solution.py:328
  28.2 6.6 %collective-permute-start.7 = (f32[264,128]{1,0:T(8,128)S(1)}, f32[264,128]{1,0:T(8,128)S(1)}, u32[]{:S(2)}, u32[]{:S(2)}) collective-permute-start(f32[264,128]{1,0:T(8,128)S(1)} %get-tuple-element.29), channel_id=1, source_target_pairs={{0,1},{1,0},{2,3},{3,2},{4,5},{5,4},{6,7},{7,6},{8,9},{9,8},{10,11... | collective-permute-start | bytes 405512 | tf_op jit(solution)/shard_map/ppermute | solution.py:328
  29.6 7.3 %collective-permute-start.6 = (f32[264,128]{1,0:T(8,128)S(1)}, f32[264,128]{1,0:T(8,128)S(1)}, u32[]{:S(2)}, u32[]{:S(2)}) collective-permute-start(f32[264,128]{1,0:T(8,128)S(1)} %get-tuple-element.27), channel_id=1, source_target_pairs={{0,3},{1,2},{2,1},{3,0},{4,7},{5,6},{6,5},{7,4},{8,11},{9,10},{10,... | collective-permute-start | bytes 405512 | tf_op jit(solution)/shard_map/ppermute | solution.py:328

commit v2 on v1

--- a/solution.py
+++ b/solution.py
@@ -126,17 +126,15 @@
     key_dim = k_ref.shape[1] // heads
     value_dim = v_ref.shape[1] // heads
     parts = value_dim // LANES
-    copies[0].wait()
+    for copy in copies:
+        copy.wait()
     cumul = cumulative_rows(log_forget(fo_ref[...]))
-    copies[1].wait()
     level = in_ref[...] - cumul
     level_top = jnp.max(level, axis=1, keepdims=True)
     decay = cumul[:, length - 1 : length]
     scalar_ref[0] = jnp.exp(level - level_top)
     scalar_ref[1] = jnp.broadcast_to(decay + level_top, (heads, length))
     scalar_ref[2] = jnp.broadcast_to(decay, (heads, length))
-    copies[2].wait()
-    copies[3].wait()
     for head, out_ref in zip(partners(heads), out_refs):
         keys = k_ref[:, pl.ds(pl.multiple_of(head * key_dim, LANES), key_dim)]
         values = v_ref[:, pl.ds(pl.multiple_of(head * value_dim, LANES), value_dim)]
@@ -221,12 +219,23 @@
     places = partners(quad)
     me = lax.axis_index(AXES[0])
     even = (me & 1) == 0
-    start = nothing(load(within_ref))
-    for group in range(2 * own_ref.shape[0] - 1):
-        same = even if group % 2 == 0 else jnp.logical_not(even)
-        own, other = load(own_ref.at[group // 2]), load(other_ref.at[group // 2])
-        start = choose(group < me, join(start, choose(same, own, other)), start)
-    start = join(start, load(within_ref))
+    within = load(within_ref)
+    sums = [(load(own_ref.at[pair]), load(other_ref.at[pair])) for pair in range(own_ref.shape[0])]
+    tops, decays, earlier = [], [], []
+    for own, other in sums:
+        for one, two in ((own, other), (other, own)):
+            before = len(tops) < me
+            tops.append(jnp.where(before, jnp.where(even, one[2], two[2]), floor_value))
+            decays.append(jnp.where(before, jnp.where(even, one[3], two[3]), 0.0))
+            earlier.append(before)
+    weights, top, _ = weights_of(tops + [within[2]], decays + [within[3]])
+    weights[:-1] = [jnp.where(before, w, 0.0) for before, w in zip(earlier, weights)]
+    terms = [(weights[-1], within)]
+    for pair, (own, other) in enumerate(sums):
+        one, two = weights[2 * pair], weights[2 * pair + 1]
+        terms.append((jnp.where(even, one, two), own))
+        terms.append((jnp.where(even, two, one), other))
+    start = (*weighted_sum(*zip(*terms)), top)
     tops, decays = read_scalars(pieces, scalar_ref, places)
     zero = jnp.zeros_like(tops[0])
     for place in range(quad):
@@ -392,13 +401,14 @@
     )(sums, swap(sums, AXES[0], 1), *within, *pieces)
     carried = exchange(states)
     column = jax.ShapeDtypeStruct((length, value_dim), output.dtype)
-    columns = []
-    for steps in [(0, 1)] + [(step,) for step in range(2, heads - 1)]:
-        columns += pl.pallas_call(
+    columns = {}
+    for steps in [(0, *range(2, heads - 1)), (1,)]:
+        outs = pl.pallas_call(
             functools.partial(part_kernel, steps),
             out_shape=(column,) * len(steps),
             compiler_params=params,
         )(queries, inner_num, stats, *(carried[step] for step in steps))
+        columns.update(zip(steps, outs))
     return pl.pallas_call(
         last_kernel,
         out_shape=output,
@@ -408,7 +418,7 @@
             pltpu.SemaphoreType.DMA((heads,)),
         ],
         compiler_params=params,
-    )(queries, inner_num, stats, carried[-1], *columns)
+    )(queries, inner_num, stats, carried[-1], *(columns[step] for step in range(heads - 1)))
 
 
 def solution(mesh):

time: 38.1 us -> 39.1 us (1.026)
  waiting for transfers between devices: 20.3 us -> 21.1 us
    ppermute x9, waiting for transfers between devices: 20.3 us -> 21.1 us  [swap(): lax.ppermute(array, axis, [(place, place ^ step) for place in range(count)])]
  transfers between devices with their start and end apart: 9 -> 9, of which waited for: 8 -> 9; matrix products, arithmetic and copies ran while one was open for 0% -> 0% of each run, Pallas kernels for 5% -> 5%
where the time goes in v2:
time: 39.1 us; the launch traced here: 39 us
  waiting for transfers between devices  21.1 us (54%)
  starting transfers between devices  12.6 us (32%)
  Pallas kernels  5.09 us (13%)
    ppermute x9, waiting for transfers between devices, swap(): lax.ppermute(array, axis, [(place, place ^ step) for place in range(count)])  21.1 us
    ppermute x9, starting transfers between devices, swap(): lax.ppermute(array, axis, [(place, place ^ step) for place in range(count)])  12.6 us
    pallas_call x1, Pallas kernels, on_device(): pl.pallas_call(state_kernel, out_shape=messages, in_specs=[hbm] * len(ope...  1.66 us
    pallas_call x1, Pallas kernels, on_device(): pl.pallas_call(last_kernel, out_shape=output, out_specs=hbm, scratch_shap...  1.07 us
    pallas_call x2, Pallas kernels, on_device(): pl.pallas_call(functools.partial(part_kernel, steps), out_shape=(column,)...  0.99 us
    pallas_call x1, Pallas kernels, on_device(): pl.pallas_call(inner_kernel, out_shape=(jax.ShapeDtypeStruct((heads, leng...  0.87 us
  transfers between devices with their start and end apart: 9, of which 9 were waited for; matrix products, arithmetic and copies ran while one was open for 0% of the time, Pallas kernels for 5%

profile of v2, /device:TPU:0, one launch (start us, length us, event | category | flops | bytes accessed | tf_op | source)
XLA Modules:
  0.0 39.0 jit_solution(13878354021550537401)
XLA Ops:
  0.0 1.7 %shard_map.56 = (f32[264,128]{1,0:T(8,128)S(1)}, f32[264,128]{1,0:T(8,128)S(1)}, f32[264,128]{1,0:T(8,128)S(1)}, f32[264,128]{1,0:T(8,128)S(1)}) custom-call(bf16[128,512]{1,0:T(8,128)(2,1)} %k_hbm.1, bf16[128,1024]{1,0:T(8,128)(2,1)} %v_hbm.1, f32[4,128]{1,0:T(4,128)} %in_hbm.1, f32[4,128]{1,0:T(4,128)} %fo_hbm.1), custom_call_target="tpu_custom_call" | custom-call | tf_op jit(solution)/shard_map/pallas_call | solution.py:357
  1.7 3.0 %collective-permute-start = (f32[264,128]{1,0:T(8,128)S(1)}, f32[264,128]{1,0:T(8,128)S(1)}, u32[]{:S(2)}, u32[]{:S(2)}) collective-permute-start(f32[264,128]{1,0:T(8,128)S(1)} %get-tuple-element.22), channel_id=1, source_target_pairs={{0,1},{1,0},{2,3},{3,2},{4,5},{5,4},{6,7},{7,6},{8,9},{9,8},{10,11... | collective-permute-start | bytes 405512 | tf_op jit(solution)/shard_map/ppermute | solution.py:337
  4.7 1.6 %collective-permute-start.1 = (f32[264,128]{1,0:T(8,128)S(1)}, f32[264,128]{1,0:T(8,128)S(1)}, u32[]{:S(2)}, u32[]{:S(2)}) collective-permute-start(f32[264,128]{1,0:T(8,128)S(1)} %get-tuple-element.23), channel_id=1, source_target_pairs={{0,2},{1,3},{2,0},{3,1},{4,6},{5,7},{6,4},{7,5},{8,10},{9,11},{10,... | collective-permute-start | bytes 405512 | tf_op jit(solution)/shard_map/ppermute | solution.py:337
  6.3 0.0 collective-permute-start.2
  6.3 2.0 %collective-permute-done.refs_1_ = f32[264,128]{1,0:T(8,128)S(1)} collective-permute-done((f32[264,128]{1,0:T(8,128)S(1)}, f32[264,128]{1,0:T(8,128)S(1)}, u32[]{:S(2)}, u32[]{:S(2)}) %collective-permute-start) | collective-permute-done | bytes 135200 | tf_op jit(solution)/shard_map/ppermute | solution.py:337
  8.3 2.9 %collective-permute-done.1.refs_2_ = f32[264,128]{1,0:T(8,128)S(1)} collective-permute-done((f32[264,128]{1,0:T(8,128)S(1)}, f32[264,128]{1,0:T(8,128)S(1)}, u32[]{:S(2)}, u32[]{:S(2)}) %collective-permute-start.1) | collective-permute-done | bytes 135200 | tf_op jit(solution)/shard_map/ppermute | solution.py:337
  11.2 1.2 %collective-permute-done.2.refs_3_ = f32[264,128]{1,0:T(8,128)S(1)} collective-permute-done((f32[264,128]{1,0:T(8,128)S(1)}, f32[264,128]{1,0:T(8,128)S(1)}, u32[]{:S(2)}, u32[]{:S(2)}) %collective-permute-start.2) | collective-permute-done | bytes 135200 | tf_op jit(solution)/shard_map/ppermute | solution.py:337
  12.4 0.1 shard_map.57.refs_0_
  12.5 2.8 %collective-permute-start.3 = (f32[264,128]{1,0:T(8,128)S(1)}, f32[264,128]{1,0:T(8,128)S(1)}, u32[]{:S(2)}, u32[]{:S(2)}) collective-permute-start(f32[264,128]{1,0:T(8,128)S(1)} %shard_map.57.refs_0_), channel_id=1, source_target_pairs={{0,4},{1,5},{2,6},{3,7},{4,0},{5,1},{6,2},{7,3},{8,12},{9,13},{10,... | collective-permute-start | bytes 405512 | tf_op jit(solution)/shard_map/ppermute | solution.py:337
  15.3 5.6 %collective-permute-done.3.refs_1_ = f32[264,128]{1,0:T(8,128)S(1)} collective-permute-done((f32[264,128]{1,0:T(8,128)S(1)}, f32[264,128]{1,0:T(8,128)S(1)}, u32[]{:S(2)}, u32[]{:S(2)}) %collective-permute-start.3) | collective-permute-done | bytes 135200 | tf_op jit(solution)/shard_map/ppermute | solution.py:337
  21.0 0.1 shard_map.58
  21.0 1.6 %collective-permute-start.4 = (f32[264,128]{1,0:T(8,128)S(1)}, f32[264,128]{1,0:T(8,128)S(1)}, u32[]{:S(2)}, u32[]{:S(2)}) collective-permute-start(f32[264,128]{1,0:T(8,128)S(1)} %get-tuple-element.25.own_ref), channel_id=1, source_target_pairs={{0,16},{8,24},{16,0},{24,8},{1,17},{9,25},{17,1},{25,9},{2,18},{10... | collective-permute-start | bytes 405512 | tf_op jit(solution)/shard_map/ppermute | solution.py:337
  22.6 3.5 %collective-permute-done.4.other_ref = f32[264,128]{1,0:T(8,128)S(1)} collective-permute-done((f32[264,128]{1,0:T(8,128)S(1)}, f32[264,128]{1,0:T(8,128)S(1)}, u32[]{:S(2)}, u32[]{:S(2)}) %collective-permute-start.4) | collective-permute-done | bytes 135200 | tf_op jit(solution)/shard_map/ppermute | solution.py:337
  26.2 0.1 collective-permute-start.5
  26.2 1.5 %collective-permute-done.5.other_ref = f32[2,264,128]{2,1,0:T(8,128)S(1)} collective-permute-done((f32[2,264,128]{2,1,0:T(8,128)S(1)}, f32[2,264,128]{2,1,0:T(8,128)S(1)}, u32[]{:S(2)}, u32[]{:S(2)}) %collective-permute-start.5) | collective-permute-done | bytes 270368 | tf_op jit(solution)/shard_map/ppermute | solution.py:337
  27.8 0.0 copy-start
  27.8 0.0 copy-start.1
  27.8 0.0 copy-start.2
  27.8 0.3 shard_map.60
  28.1 0.0 copy-start.4
  28.1 0.0 copy-start.3
  28.1 1.0 %collective-permute-start.8 = (f32[264,128]{1,0:T(8,128)S(1)}, f32[264,128]{1,0:T(8,128)S(1)}, u32[]{:S(2)}, u32[]{:S(2)}) collective-permute-start(f32[264,128]{1,0:T(8,128)S(1)} %get-tuple-element.31), channel_id=1, source_target_pairs={{0,1},{1,0},{2,3},{3,2},{4,5},{5,4},{6,7},{7,6},{8,9},{9,8},{10,11... | collective-permute-start | bytes 405512 | tf_op jit(solution)/shard_map/ppermute | solution.py:337
  29.1 0.7 %collective-permute-start.7 = (f32[264,128]{1,0:T(8,128)S(1)}, f32[264,128]{1,0:T(8,128)S(1)}, u32[]{:S(2)}, u32[]{:S(2)}) collective-permute-start(f32[264,128]{1,0:T(8,128)S(1)} %get-tuple-element.29), channel_id=1, source_target_pairs={{0,2},{1,3},{2,0},{3,1},{4,6},{5,7},{6,4},{7,5},{8,10},{9,11},{10,... | collective-permute-start | bytes 405512 | tf_op jit(solution)/shard_map/ppermute | solution.py:337
  29.8 1.9 %collective-permute-start.6 = (f32[264,128]{1,0:T(8,128)S(1)}, f32[264,128]{1,0:T(8,128)S(1)}, u32[]{:S(2)}, u32[]{:S(2)}) collective-permute-start(f32[264,128]{1,0:T(8,128)S(1)} %get-tuple-element.27), channel_id=1, source_target_pairs={{0,3},{1,2},{2,1},{3,0},{4,7},{5,6},{6,5},{7,4},{8,11},{9,10},{10,... | collective-permute-start | bytes 405512 | tf_op jit(solution)/shard_map/ppermute | solution.py:337
  31.7 0.0 copy-done
  31.7 0.0 copy-done.1
  31.7 0.0 copy-done.2
  31.7 0.0 copy-done.4
  31.7 0.0 copy-done.3
  31.7 0.9 %shard_map.55 = (f32[4,128,256]{2,1,0:T(8,128)S(1)}, f32[4,128,3]{2,1,0:T(8,128)S(1)}) custom-call(bf16[128,512]{1,0:T(8,128)(2,1)S(1)} %copy-done, bf16[128,512]{1,0:T(8,128)(2,1)S(1)} %copy-done.2, bf16[128,1024]{1,0:T(8,128)(2,1)S(1)} %copy-done.1, f32[4,128]{1,0:T(4,128)S(1)} %copy-done.3, f32[4,128]{1,0:T(4,128)S(1)} %copy-done.4), custom_call_target="tpu_custom_call" | custom-call | tf_op jit(solution)/shard_map/pallas_call | solution.py:366
  32.6 1.2 %collective-permute-done.8.refs_0_ = f32[264,128]{1,0:T(8,128)S(1)} collective-permute-done((f32[264,128]{1,0:T(8,128)S(1)}, f32[264,128]{1,0:T(8,128)S(1)}, u32[]{:S(2)}, u32[]{:S(2)}) %collective-permute-start.8) | collective-permute-done | bytes 135200 | tf_op jit(solution)/shard_map/ppermute | solution.py:337
  33.8 0.4 %shard_map.62.refs_1_ = bf16[128,256]{1,0:T(8,128)(2,1)S(1)} custom-call(bf16[128,512]{1,0:T(8,128)(2,1)S(1)} %copy-done, f32[4,128,256]{2,1,0:T(8,128)S(1)} %get-tuple-element.19.num_ref, f32[4,128,3]{2,1,0:T(8,128)S(1)} %get-tuple-element.20.stat_ref, f32[264,128]{1,0:T(8,128)S(1)} %collective-permute-done.8.refs_0_), custom_call_target="tpu_custom_call" | custom-call | tf_op jit(solution)/shard_map/pallas_call | solution.py:406
  34.2 1.3 %collective-permute-done.7.refs_1_ = f32[264,128]{1,0:T(8,128)S(1)} collective-permute-done((f32[264,128]{1,0:T(8,128)S(1)}, f32[264,128]{1,0:T(8,128)S(1)}, u32[]{:S(2)}, u32[]{:S(2)}) %collective-permute-start.7) | collective-permute-done | bytes 135200 | tf_op jit(solution)/shard_map/ppermute | solution.py:337
  35.6 0.6 %shard_map.61 = (bf16[128,256]{1,0:T(8,128)(2,1)S(1)}, bf16[128,256]{1,0:T(8,128)(2,1)S(1)}) custom-call(bf16[128,512]{1,0:T(8,128)(2,1)S(1)} %copy-done, f32[4,128,256]{2,1,0:T(8,128)S(1)} %get-tuple-element.19.num_ref, f32[4,128,3]{2,1,0:T(8,128)S(1)} %get-tuple-element.20.stat_ref, f32[264,128]{1,0:T(8,128)S(1)} %get-tuple-element.28.refs_0_, ...), custom_call_target="tpu_custom_call" | custom-call | tf_op jit(solution)/shard_map/pallas_call | solution.py:406
  36.2 1.7 %collective-permute-done.6.message_ref = f32[264,128]{1,0:T(8,128)S(1)} collective-permute-done((f32[264,128]{1,0:T(8,128)S(1)}, f32[264,128]{1,0:T(8,128)S(1)}, u32[]{:S(2)}, u32[]{:S(2)}) %collective-permute-start.6) | collective-permute-done | bytes 135200 | tf_op jit(solution)/shard_map/ppermute | solution.py:337
  37.9 1.1 %shard_map.63 = bf16[128,1024]{1,0:T(8,128)(2,1)} custom-call(bf16[128,512]{1,0:T(8,128)(2,1)S(1)} %copy-done, f32[4,128,256]{2,1,0:T(8,128)S(1)} %get-tuple-element.19.num_ref, f32[4,128,3]{2,1,0:T(8,128)S(1)} %get-tuple-element.20.stat_ref, f32[264,128]{1,0:T(8,128)S(1)} %collective-permute-done.6.message_ref, ...), custom_call_target="tpu_custom_call" | custom-call | tf_op jit(solution)/shard_map/pallas_call | solution.py:412
  (1 shorter events, 0.0 us)
Async XLA Ops:
  1.7 6.6 %collective-permute-start = (f32[264,128]{1,0:T(8,128)S(1)}, f32[264,128]{1,0:T(8,128)S(1)}, u32[]{:S(2)}, u32[]{:S(2)}) collective-permute-start(f32[264,128]{1,0:T(8,128)S(1)} %get-tuple-element.22), channel_id=1, source_target_pairs={{0,1},{1,0},{2,3},{3,2},{4,5},{5,4},{6,7},{7,6},{8,9},{9,8},{10,11... | collective-permute-start | bytes 405512 | tf_op jit(solution)/shard_map/ppermute | solution.py:337
  4.7 6.5 %collective-permute-start.1 = (f32[264,128]{1,0:T(8,128)S(1)}, f32[264,128]{1,0:T(8,128)S(1)}, u32[]{:S(2)}, u32[]{:S(2)}) collective-permute-start(f32[264,128]{1,0:T(8,128)S(1)} %get-tuple-element.23), channel_id=1, source_target_pairs={{0,2},{1,3},{2,0},{3,1},{4,6},{5,7},{6,4},{7,5},{8,10},{9,11},{10,... | collective-permute-start | bytes 405512 | tf_op jit(solution)/shard_map/ppermute | solution.py:337
  6.3 6.2 %collective-permute-start.2 = (f32[264,128]{1,0:T(8,128)S(1)}, f32[264,128]{1,0:T(8,128)S(1)}, u32[]{:S(2)}, u32[]{:S(2)}) collective-permute-start(f32[264,128]{1,0:T(8,128)S(1)} %get-tuple-element.24), channel_id=1, source_target_pairs={{0,3},{1,2},{2,1},{3,0},{4,7},{5,6},{6,5},{7,4},{8,11},{9,10},{10,... | collective-permute-start | bytes 405512 | tf_op jit(solution)/shard_map/ppermute | solution.py:337
  12.5 8.4 %collective-permute-start.3 = (f32[264,128]{1,0:T(8,128)S(1)}, f32[264,128]{1,0:T(8,128)S(1)}, u32[]{:S(2)}, u32[]{:S(2)}) collective-permute-start(f32[264,128]{1,0:T(8,128)S(1)} %shard_map.57.refs_0_), channel_id=1, source_target_pairs={{0,4},{1,5},{2,6},{3,7},{4,0},{5,1},{6,2},{7,3},{8,12},{9,13},{10,... | collective-permute-start | bytes 405512 | tf_op jit(solution)/shard_map/ppermute | solution.py:337
  21.0 5.1 %collective-permute-start.4 = (f32[264,128]{1,0:T(8,128)S(1)}, f32[264,128]{1,0:T(8,128)S(1)}, u32[]{:S(2)}, u32[]{:S(2)}) collective-permute-start(f32[264,128]{1,0:T(8,128)S(1)} %get-tuple-element.25.own_ref), channel_id=1, source_target_pairs={{0,16},{8,24},{16,0},{24,8},{1,17},{9,25},{17,1},{25,9},{2,18},{10... | collective-permute-start | bytes 405512 | tf_op jit(solution)/shard_map/ppermute | solution.py:337
  26.2 1.6 %collective-permute-start.5 = (f32[2,264,128]{2,1,0:T(8,128)S(1)}, f32[2,264,128]{2,1,0:T(8,128)S(1)}, u32[]{:S(2)}, u32[]{:S(2)}) collective-permute-start(f32[2,264,128]{2,1,0:T(8,128)S(1)} %shard_map.59.own_ref), channel_id=1, source_target_pairs={{0,8},{8,0},{16,24},{24,16},{1,9},{9,1},{17,25},{25,17},{2,10},{10... | collective-permute-start | bytes 811016 | tf_op jit(solution)/shard_map/ppermute | solution.py:337
  27.8 3.9 %copy-start = (bf16[128,512]{1,0:T(8,128)(2,1)S(1)}, bf16[128,512]{1,0:T(8,128)(2,1)}, u32[]{:S(2)}) copy-start(bf16[128,512]{1,0:T(8,128)(2,1)} %q_ref.7) | copy-start | bytes 393220
  27.8 3.9 %copy-start.1 = (bf16[128,1024]{1,0:T(8,128)(2,1)S(1)}, bf16[128,1024]{1,0:T(8,128)(2,1)}, u32[]{:S(2)}) copy-start(bf16[128,1024]{1,0:T(8,128)(2,1)} %v_hbm.1) | copy-start | bytes 786436
  27.8 3.9 %copy-start.2 = (bf16[128,512]{1,0:T(8,128)(2,1)S(1)}, bf16[128,512]{1,0:T(8,128)(2,1)}, u32[]{:S(2)}) copy-start(bf16[128,512]{1,0:T(8,128)(2,1)} %k_hbm.1) | copy-start | bytes 393220
  28.1 3.6 %copy-start.4 = (f32[4,128]{1,0:T(4,128)S(1)}, f32[4,128]{1,0:T(4,128)}, u32[]{:S(2)}) copy-start(f32[4,128]{1,0:T(4,128)} %fo_hbm.1) | copy-start | bytes 6148
  28.1 3.6 %copy-start.3 = (f32[4,128]{1,0:T(4,128)S(1)}, f32[4,128]{1,0:T(4,128)}, u32[]{:S(2)}) copy-start(f32[4,128]{1,0:T(4,128)} %in_hbm.1) | copy-start | bytes 6148
  28.1 5.7 %collective-permute-start.8 = (f32[264,128]{1,0:T(8,128)S(1)}, f32[264,128]{1,0:T(8,128)S(1)}, u32[]{:S(2)}, u32[]{:S(2)}) collective-permute-start(f32[264,128]{1,0:T(8,128)S(1)} %get-tuple-element.31), channel_id=1, source_target_pairs={{0,1},{1,0},{2,3},{3,2},{4,5},{5,4},{6,7},{7,6},{8,9},{9,8},{10,11... | collective-permute-start | bytes 405512 | tf_op jit(solution)/shard_map/ppermute | solution.py:337
  29.1 6.5 %collective-permute-start.7 = (f32[264,128]{1,0:T(8,128)S(1)}, f32[264,128]{1,0:T(8,128)S(1)}, u32[]{:S(2)}, u32[]{:S(2)}) collective-permute-start(f32[264,128]{1,0:T(8,128)S(1)} %get-tuple-element.29), channel_id=1, source_target_pairs={{0,2},{1,3},{2,0},{3,1},{4,6},{5,7},{6,4},{7,5},{8,10},{9,11},{10,... | collective-permute-start | bytes 405512 | tf_op jit(solution)/shard_map/ppermute | solution.py:337
  29.8 8.1 %collective-permute-start.6 = (f32[264,128]{1,0:T(8,128)S(1)}, f32[264,128]{1,0:T(8,128)S(1)}, u32[]{:S(2)}, u32[]{:S(2)}) collective-permute-start(f32[264,128]{1,0:T(8,128)S(1)} %get-tuple-element.27), channel_id=1, source_target_pairs={{0,3},{1,2},{2,1},{3,0},{4,7},{5,6},{6,5},{7,4},{8,11},{9,10},{10,... | collective-permute-start | bytes 405512 | tf_op jit(solution)/shard_map/ppermute | solution.py:337

commit v3 on v2

--- a/solution.py
+++ b/solution.py
@@ -64,8 +64,12 @@
     return lax.rem(lax.axis_index(AXES[1]), quad)
 
 
+def distances(quad):
+    return [0, *range(quad - 2, 0, -1), quad - 1]
+
+
 def partners(quad):
-    return [member(quad) ^ step for step in range(quad)]
+    return [member(quad) ^ distance for distance in distances(quad)]
 
 
 def tail_rows(vector, top, decay):
@@ -126,15 +130,17 @@
     key_dim = k_ref.shape[1] // heads
     value_dim = v_ref.shape[1] // heads
     parts = value_dim // LANES
-    for copy in copies:
-        copy.wait()
+    copies[0].wait()
     cumul = cumulative_rows(log_forget(fo_ref[...]))
+    copies[1].wait()
     level = in_ref[...] - cumul
     level_top = jnp.max(level, axis=1, keepdims=True)
     decay = cumul[:, length - 1 : length]
     scalar_ref[0] = jnp.exp(level - level_top)
     scalar_ref[1] = jnp.broadcast_to(decay + level_top, (heads, length))
     scalar_ref[2] = jnp.broadcast_to(decay, (heads, length))
+    copies[2].wait()
+    copies[3].wait()
     for head, out_ref in zip(partners(heads), out_refs):
         keys = k_ref[:, pl.ds(pl.multiple_of(head * key_dim, LANES), key_dim)]
         values = v_ref[:, pl.ds(pl.multiple_of(head * value_dim, LANES), value_dim)]
@@ -338,7 +344,8 @@
 
 
 def exchange(pieces):
-    return [pieces[0]] + [swap(pieces[step], AXES[1], step) for step in range(1, len(pieces))]
+    steps = zip(pieces[1:], distances(len(pieces))[1:])
+    return [pieces[0]] + [swap(piece, AXES[1], distance) for piece, distance in steps]
 
 
 def on_device(groups, group_length, queries, key_vectors, value_vectors, input_gate, forget_gate):

time: 39.1 us -> 38.5 us (0.985)
  transfers between devices with their start and end apart: 9 -> 9, of which waited for: 9 -> 8; matrix products, arithmetic and copies ran while one was open for 0% -> 0% of each run, Pallas kernels for 5% -> 5%
where the time goes in v3:
time: 38.5 us; the launch traced here: 38.3 us
  waiting for transfers between devices  20.9 us (54%)
  starting transfers between devices  12.5 us (32%)
  Pallas kernels  4.87 us (13%)
    ppermute x9, waiting for transfers between devices, swap(): lax.ppermute(array, axis, [(place, place ^ step) for place in range(count)])  20.9 us
    ppermute x9, starting transfers between devices, swap(): lax.ppermute(array, axis, [(place, place ^ step) for place in range(count)])  12.5 us
    pallas_call x1, Pallas kernels, on_device(): pl.pallas_call(state_kernel, out_shape=messages, in_specs=[hbm] * len(ope...  1.44 us
    pallas_call x1, Pallas kernels, on_device(): pl.pallas_call(last_kernel, out_shape=output, out_specs=hbm, scratch_shap...  1.08 us
    pallas_call x2, Pallas kernels, on_device(): pl.pallas_call(functools.partial(part_kernel, steps), out_shape=(column,)...  0.99 us
    pallas_call x1, Pallas kernels, on_device(): pl.pallas_call(inner_kernel, out_shape=(jax.ShapeDtypeStruct((heads, leng...  0.88 us
  transfers between devices with their start and end apart: 9, of which 8 were waited for; matrix products, arithmetic and copies ran while one was open for 0% of the time, Pallas kernels for 5%

profile of v3, /device:TPU:0, one launch (start us, length us, event | category | flops | bytes accessed | tf_op | source)
XLA Modules:
  0.0 38.3 jit_solution(2165936325025472662)
XLA Ops:
  0.0 1.4 %shard_map.56 = (f32[264,128]{1,0:T(8,128)S(1)}, f32[264,128]{1,0:T(8,128)S(1)}, f32[264,128]{1,0:T(8,128)S(1)}, f32[264,128]{1,0:T(8,128)S(1)}) custom-call(bf16[128,512]{1,0:T(8,128)(2,1)} %k_hbm.1, bf16[128,1024]{1,0:T(8,128)(2,1)} %v_hbm.1, f32[4,128]{1,0:T(4,128)} %in_hbm.1, f32[4,128]{1,0:T(4,128)} %fo_hbm.1), custom_call_target="tpu_custom_call" | custom-call | tf_op jit(solution)/shard_map/pallas_call | solution.py:364
  1.5 3.1 %collective-permute-start = (f32[264,128]{1,0:T(8,128)S(1)}, f32[264,128]{1,0:T(8,128)S(1)}, u32[]{:S(2)}, u32[]{:S(2)}) collective-permute-start(f32[264,128]{1,0:T(8,128)S(1)} %get-tuple-element.22), channel_id=1, source_target_pairs={{0,2},{1,3},{2,0},{3,1},{4,6},{5,7},{6,4},{7,5},{8,10},{9,11},{10,... | collective-permute-start | bytes 405512 | tf_op jit(solution)/shard_map/ppermute | solution.py:343
  4.5 1.5 %collective-permute-start.1 = (f32[264,128]{1,0:T(8,128)S(1)}, f32[264,128]{1,0:T(8,128)S(1)}, u32[]{:S(2)}, u32[]{:S(2)}) collective-permute-start(f32[264,128]{1,0:T(8,128)S(1)} %get-tuple-element.23), channel_id=1, source_target_pairs={{0,1},{1,0},{2,3},{3,2},{4,5},{5,4},{6,7},{7,6},{8,9},{9,8},{10,11... | collective-permute-start | bytes 405512 | tf_op jit(solution)/shard_map/ppermute | solution.py:343
  6.1 0.0 collective-permute-start.2
  6.1 2.5 %collective-permute-done.refs_1_ = f32[264,128]{1,0:T(8,128)S(1)} collective-permute-done((f32[264,128]{1,0:T(8,128)S(1)}, f32[264,128]{1,0:T(8,128)S(1)}, u32[]{:S(2)}, u32[]{:S(2)}) %collective-permute-start) | collective-permute-done | bytes 135200 | tf_op jit(solution)/shard_map/ppermute | solution.py:343
  8.5 4.0 %collective-permute-done.1.refs_2_ = f32[264,128]{1,0:T(8,128)S(1)} collective-permute-done((f32[264,128]{1,0:T(8,128)S(1)}, f32[264,128]{1,0:T(8,128)S(1)}, u32[]{:S(2)}, u32[]{:S(2)}) %collective-permute-start.1) | collective-permute-done | bytes 135200 | tf_op jit(solution)/shard_map/ppermute | solution.py:343
  12.5 0.0 collective-permute-done.2.refs_3_
  12.5 0.1 shard_map.57.refs_0_
  12.6 2.7 %collective-permute-start.3 = (f32[264,128]{1,0:T(8,128)S(1)}, f32[264,128]{1,0:T(8,128)S(1)}, u32[]{:S(2)}, u32[]{:S(2)}) collective-permute-start(f32[264,128]{1,0:T(8,128)S(1)} %shard_map.57.refs_0_), channel_id=1, source_target_pairs={{0,4},{1,5},{2,6},{3,7},{4,0},{5,1},{6,2},{7,3},{8,12},{9,13},{10,... | collective-permute-start | bytes 405512 | tf_op jit(solution)/shard_map/ppermute | solution.py:343
  15.2 5.2 %collective-permute-done.3.refs_1_ = f32[264,128]{1,0:T(8,128)S(1)} collective-permute-done((f32[264,128]{1,0:T(8,128)S(1)}, f32[264,128]{1,0:T(8,128)S(1)}, u32[]{:S(2)}, u32[]{:S(2)}) %collective-permute-start.3) | collective-permute-done | bytes 135200 | tf_op jit(solution)/shard_map/ppermute | solution.py:343
  20.4 0.1 shard_map.58
  20.5 1.6 %collective-permute-start.4 = (f32[264,128]{1,0:T(8,128)S(1)}, f32[264,128]{1,0:T(8,128)S(1)}, u32[]{:S(2)}, u32[]{:S(2)}) collective-permute-start(f32[264,128]{1,0:T(8,128)S(1)} %get-tuple-element.25.own_ref), channel_id=1, source_target_pairs={{0,16},{8,24},{16,0},{24,8},{1,17},{9,25},{17,1},{25,9},{2,18},{10... | collective-permute-start | bytes 405512 | tf_op jit(solution)/shard_map/ppermute | solution.py:343
  22.0 3.5 %collective-permute-done.4.other_ref = f32[264,128]{1,0:T(8,128)S(1)} collective-permute-done((f32[264,128]{1,0:T(8,128)S(1)}, f32[264,128]{1,0:T(8,128)S(1)}, u32[]{:S(2)}, u32[]{:S(2)}) %collective-permute-start.4) | collective-permute-done | bytes 135200 | tf_op jit(solution)/shard_map/ppermute | solution.py:343
  25.6 0.1 collective-permute-start.5
  25.6 1.5 %collective-permute-done.5.other_ref = f32[2,264,128]{2,1,0:T(8,128)S(1)} collective-permute-done((f32[2,264,128]{2,1,0:T(8,128)S(1)}, f32[2,264,128]{2,1,0:T(8,128)S(1)}, u32[]{:S(2)}, u32[]{:S(2)}) %collective-permute-start.5) | collective-permute-done | bytes 270368 | tf_op jit(solution)/shard_map/ppermute | solution.py:343
  27.2 0.0 copy-start
  27.2 0.0 copy-start.1
  27.2 0.0 copy-start.2
  27.2 0.3 shard_map.60
  27.5 0.0 copy-start.4
  27.5 0.0 copy-start.3
  27.5 0.7 %collective-permute-start.8 = (f32[264,128]{1,0:T(8,128)S(1)}, f32[264,128]{1,0:T(8,128)S(1)}, u32[]{:S(2)}, u32[]{:S(2)}) collective-permute-start(f32[264,128]{1,0:T(8,128)S(1)} %get-tuple-element.31), channel_id=1, source_target_pairs={{0,2},{1,3},{2,0},{3,1},{4,6},{5,7},{6,4},{7,5},{8,10},{9,11},{10,... | collective-permute-start | bytes 405512 | tf_op jit(solution)/shard_map/ppermute | solution.py:343
  28.3 1.1 %collective-permute-start.7 = (f32[264,128]{1,0:T(8,128)S(1)}, f32[264,128]{1,0:T(8,128)S(1)}, u32[]{:S(2)}, u32[]{:S(2)}) collective-permute-start(f32[264,128]{1,0:T(8,128)S(1)} %get-tuple-element.29), channel_id=1, source_target_pairs={{0,1},{1,0},{2,3},{3,2},{4,5},{5,4},{6,7},{7,6},{8,9},{9,8},{10,11... | collective-permute-start | bytes 405512 | tf_op jit(solution)/shard_map/ppermute | solution.py:343
  29.4 1.7 %collective-permute-start.6 = (f32[264,128]{1,0:T(8,128)S(1)}, f32[264,128]{1,0:T(8,128)S(1)}, u32[]{:S(2)}, u32[]{:S(2)}) collective-permute-start(f32[264,128]{1,0:T(8,128)S(1)} %get-tuple-element.27), channel_id=1, source_target_pairs={{0,3},{1,2},{2,1},{3,0},{4,7},{5,6},{6,5},{7,4},{8,11},{9,10},{10,... | collective-permute-start | bytes 405512 | tf_op jit(solution)/shard_map/ppermute | solution.py:343
  31.1 0.0 copy-done
  31.1 0.0 copy-done.1
  31.1 0.0 copy-done.2
  31.1 0.0 copy-done.4
  31.1 0.0 copy-done.3
  31.1 0.9 %shard_map.55 = (f32[4,128,256]{2,1,0:T(8,128)S(1)}, f32[4,128,3]{2,1,0:T(8,128)S(1)}) custom-call(bf16[128,512]{1,0:T(8,128)(2,1)S(1)} %copy-done, bf16[128,512]{1,0:T(8,128)(2,1)S(1)} %copy-done.2, bf16[128,1024]{1,0:T(8,128)(2,1)S(1)} %copy-done.1, f32[4,128]{1,0:T(4,128)S(1)} %copy-done.3, f32[4,128]{1,0:T(4,128)S(1)} %copy-done.4), custom_call_target="tpu_custom_call" | custom-call | tf_op jit(solution)/shard_map/pallas_call | solution.py:373
  32.0 2.0 %collective-permute-done.8.refs_0_ = f32[264,128]{1,0:T(8,128)S(1)} collective-permute-done((f32[264,128]{1,0:T(8,128)S(1)}, f32[264,128]{1,0:T(8,128)S(1)}, u32[]{:S(2)}, u32[]{:S(2)}) %collective-permute-start.8) | collective-permute-done | bytes 135200 | tf_op jit(solution)/shard_map/ppermute | solution.py:343
  34.0 0.4 %shard_map.62.refs_1_ = bf16[128,256]{1,0:T(8,128)(2,1)S(1)} custom-call(bf16[128,512]{1,0:T(8,128)(2,1)S(1)} %copy-done, f32[4,128,256]{2,1,0:T(8,128)S(1)} %get-tuple-element.19.num_ref, f32[4,128,3]{2,1,0:T(8,128)S(1)} %get-tuple-element.20.stat_ref, f32[264,128]{1,0:T(8,128)S(1)} %collective-permute-done.8.refs_0_), custom_call_target="tpu_custom_call" | custom-call | tf_op jit(solution)/shard_map/pallas_call | solution.py:413
  34.4 1.0 %collective-permute-done.7.refs_1_ = f32[264,128]{1,0:T(8,128)S(1)} collective-permute-done((f32[264,128]{1,0:T(8,128)S(1)}, f32[264,128]{1,0:T(8,128)S(1)}, u32[]{:S(2)}, u32[]{:S(2)}) %collective-permute-start.7) | collective-permute-done | bytes 135200 | tf_op jit(solution)/shard_map/ppermute | solution.py:343
  35.4 0.6 %shard_map.61 = (bf16[128,256]{1,0:T(8,128)(2,1)S(1)}, bf16[128,256]{1,0:T(8,128)(2,1)S(1)}) custom-call(bf16[128,512]{1,0:T(8,128)(2,1)S(1)} %copy-done, f32[4,128,256]{2,1,0:T(8,128)S(1)} %get-tuple-element.19.num_ref, f32[4,128,3]{2,1,0:T(8,128)S(1)} %get-tuple-element.20.stat_ref, f32[264,128]{1,0:T(8,128)S(1)} %get-tuple-element.28.refs_0_, ...), custom_call_target="tpu_custom_call" | custom-call | tf_op jit(solution)/shard_map/pallas_call | solution.py:413
  36.0 1.2 %collective-permute-done.6.message_ref = f32[264,128]{1,0:T(8,128)S(1)} collective-permute-done((f32[264,128]{1,0:T(8,128)S(1)}, f32[264,128]{1,0:T(8,128)S(1)}, u32[]{:S(2)}, u32[]{:S(2)}) %collective-permute-start.6) | collective-permute-done | bytes 135200 | tf_op jit(solution)/shard_map/ppermute | solution.py:343
  37.2 1.1 %shard_map.63 = bf16[128,1024]{1,0:T(8,128)(2,1)} custom-call(bf16[128,512]{1,0:T(8,128)(2,1)S(1)} %copy-done, f32[4,128,256]{2,1,0:T(8,128)S(1)} %get-tuple-element.19.num_ref, f32[4,128,3]{2,1,0:T(8,128)S(1)} %get-tuple-element.20.stat_ref, f32[264,128]{1,0:T(8,128)S(1)} %collective-permute-done.6.message_ref, ...), custom_call_target="tpu_custom_call" | custom-call | tf_op jit(solution)/shard_map/pallas_call | solution.py:419
  (1 shorter events, 0.0 us)
Async XLA Ops:
  1.5 7.1 %collective-permute-start = (f32[264,128]{1,0:T(8,128)S(1)}, f32[264,128]{1,0:T(8,128)S(1)}, u32[]{:S(2)}, u32[]{:S(2)}) collective-permute-start(f32[264,128]{1,0:T(8,128)S(1)} %get-tuple-element.22), channel_id=1, source_target_pairs={{0,2},{1,3},{2,0},{3,1},{4,6},{5,7},{6,4},{7,5},{8,10},{9,11},{10,... | collective-permute-start | bytes 405512 | tf_op jit(solution)/shard_map/ppermute | solution.py:343
  4.5 7.9 %collective-permute-start.1 = (f32[264,128]{1,0:T(8,128)S(1)}, f32[264,128]{1,0:T(8,128)S(1)}, u32[]{:S(2)}, u32[]{:S(2)}) collective-permute-start(f32[264,128]{1,0:T(8,128)S(1)} %get-tuple-element.23), channel_id=1, source_target_pairs={{0,1},{1,0},{2,3},{3,2},{4,5},{5,4},{6,7},{7,6},{8,9},{9,8},{10,11... | collective-permute-start | bytes 405512 | tf_op jit(solution)/shard_map/ppermute | solution.py:343
  6.1 6.4 %collective-permute-start.2 = (f32[264,128]{1,0:T(8,128)S(1)}, f32[264,128]{1,0:T(8,128)S(1)}, u32[]{:S(2)}, u32[]{:S(2)}) collective-permute-start(f32[264,128]{1,0:T(8,128)S(1)} %get-tuple-element.24), channel_id=1, source_target_pairs={{0,3},{1,2},{2,1},{3,0},{4,7},{5,6},{6,5},{7,4},{8,11},{9,10},{10,... | collective-permute-start | bytes 405512 | tf_op jit(solution)/shard_map/ppermute | solution.py:343
  12.6 7.8 %collective-permute-start.3 = (f32[264,128]{1,0:T(8,128)S(1)}, f32[264,128]{1,0:T(8,128)S(1)}, u32[]{:S(2)}, u32[]{:S(2)}) collective-permute-start(f32[264,128]{1,0:T(8,128)S(1)} %shard_map.57.refs_0_), channel_id=1, source_target_pairs={{0,4},{1,5},{2,6},{3,7},{4,0},{5,1},{6,2},{7,3},{8,12},{9,13},{10,... | collective-permute-start | bytes 405512 | tf_op jit(solution)/shard_map/ppermute | solution.py:343
  20.5 5.1 %collective-permute-start.4 = (f32[264,128]{1,0:T(8,128)S(1)}, f32[264,128]{1,0:T(8,128)S(1)}, u32[]{:S(2)}, u32[]{:S(2)}) collective-permute-start(f32[264,128]{1,0:T(8,128)S(1)} %get-tuple-element.25.own_ref), channel_id=1, source_target_pairs={{0,16},{8,24},{16,0},{24,8},{1,17},{9,25},{17,1},{25,9},{2,18},{10... | collective-permute-start | bytes 405512 | tf_op jit(solution)/shard_map/ppermute | solution.py:343
  25.6 1.6 %collective-permute-start.5 = (f32[2,264,128]{2,1,0:T(8,128)S(1)}, f32[2,264,128]{2,1,0:T(8,128)S(1)}, u32[]{:S(2)}, u32[]{:S(2)}) collective-permute-start(f32[2,264,128]{2,1,0:T(8,128)S(1)} %shard_map.59.own_ref), channel_id=1, source_target_pairs={{0,8},{8,0},{16,24},{24,16},{1,9},{9,1},{17,25},{25,17},{2,10},{10... | collective-permute-start | bytes 811016 | tf_op jit(solution)/shard_map/ppermute | solution.py:343
  27.2 3.9 %copy-start = (bf16[128,512]{1,0:T(8,128)(2,1)S(1)}, bf16[128,512]{1,0:T(8,128)(2,1)}, u32[]{:S(2)}) copy-start(bf16[128,512]{1,0:T(8,128)(2,1)} %q_ref.7) | copy-start | bytes 393220
  27.2 3.9 %copy-start.1 = (bf16[128,1024]{1,0:T(8,128)(2,1)S(1)}, bf16[128,1024]{1,0:T(8,128)(2,1)}, u32[]{:S(2)}) copy-start(bf16[128,1024]{1,0:T(8,128)(2,1)} %v_hbm.1) | copy-start | bytes 786436
  27.2 3.9 %copy-start.2 = (bf16[128,512]{1,0:T(8,128)(2,1)S(1)}, bf16[128,512]{1,0:T(8,128)(2,1)}, u32[]{:S(2)}) copy-start(bf16[128,512]{1,0:T(8,128)(2,1)} %k_hbm.1) | copy-start | bytes 393220
  27.5 3.6 %copy-start.4 = (f32[4,128]{1,0:T(4,128)S(1)}, f32[4,128]{1,0:T(4,128)}, u32[]{:S(2)}) copy-start(f32[4,128]{1,0:T(4,128)} %fo_hbm.1) | copy-start | bytes 6148
  27.5 3.6 %copy-start.3 = (f32[4,128]{1,0:T(4,128)S(1)}, f32[4,128]{1,0:T(4,128)}, u32[]{:S(2)}) copy-start(f32[4,128]{1,0:T(4,128)} %in_hbm.1) | copy-start | bytes 6148
  27.5 6.5 %collective-permute-start.8 = (f32[264,128]{1,0:T(8,128)S(1)}, f32[264,128]{1,0:T(8,128)S(1)}, u32[]{:S(2)}, u32[]{:S(2)}) collective-permute-start(f32[264,128]{1,0:T(8,128)S(1)} %get-tuple-element.31), channel_id=1, source_target_pairs={{0,2},{1,3},{2,0},{3,1},{4,6},{5,7},{6,4},{7,5},{8,10},{9,11},{10,... | collective-permute-start | bytes 405512 | tf_op jit(solution)/shard_map/ppermute | solution.py:343
  28.3 7.2 %collective-permute-start.7 = (f32[264,128]{1,0:T(8,128)S(1)}, f32[264,128]{1,0:T(8,128)S(1)}, u32[]{:S(2)}, u32[]{:S(2)}) collective-permute-start(f32[264,128]{1,0:T(8,128)S(1)} %get-tuple-element.29), channel_id=1, source_target_pairs={{0,1},{1,0},{2,3},{3,2},{4,5},{5,4},{6,7},{7,6},{8,9},{9,8},{10,11... | collective-permute-start | bytes 405512 | tf_op jit(solution)/shard_map/ppermute | solution.py:343
  29.4 7.9 %collective-permute-start.6 = (f32[264,128]{1,0:T(8,128)S(1)}, f32[264,128]{1,0:T(8,128)S(1)}, u32[]{:S(2)}, u32[]{:S(2)}) collective-permute-start(f32[264,128]{1,0:T(8,128)S(1)} %get-tuple-element.27), channel_id=1, source_target_pairs={{0,3},{1,2},{2,1},{3,0},{4,7},{5,6},{6,5},{7,4},{8,11},{9,10},{10,... | collective-permute-start | bytes 405512 | tf_op jit(solution)/shard_map/ppermute | solution.py:343

commit v4 on v3

--- a/solution.py
+++ b/solution.py
@@ -65,7 +65,7 @@
 
 
 def distances(quad):
-    return [0, *range(quad - 2, 0, -1), quad - 1]
+    return [0, *range(quad - 1, 0, -1)]
 
 
 def partners(quad):

time: 38.5 us -> 40.1 us (1.042)
  waiting for transfers between devices: 20.9 us -> 22.2 us
    ppermute x9, waiting for transfers between devices: 20.9 us -> 22.2 us  [swap(): lax.ppermute(array, axis, [(place, place ^ step) for place in range(count)])]
  transfers between devices with their start and end apart: 9 -> 9, of which waited for: 8 -> 7; matrix products, arithmetic and copies ran while one was open for 0% -> 0% of each run, Pallas kernels for 5% -> 5%
where the time goes in v4:
time: 40.1 us; the launch traced here: 39.9 us
  waiting for transfers between devices  22.2 us (55%)
  starting transfers between devices  12.7 us (32%)
  Pallas kernels  4.88 us (12%)
    ppermute x9, waiting for transfers between devices, swap(): lax.ppermute(array, axis, [(place, place ^ step) for place in range(count)])  22.2 us
    ppermute x9, starting transfers between devices, swap(): lax.ppermute(array, axis, [(place, place ^ step) for place in range(count)])  12.7 us
    pallas_call x1, Pallas kernels, on_device(): pl.pallas_call(state_kernel, out_shape=messages, in_specs=[hbm] * len(ope...  1.44 us
    pallas_call x1, Pallas kernels, on_device(): pl.pallas_call(last_kernel, out_shape=output, out_specs=hbm, scratch_shap...  1.08 us
    pallas_call x2, Pallas kernels, on_device(): pl.pallas_call(functools.partial(part_kernel, steps), out_shape=(column,)...  0.99 us
    pallas_call x1, Pallas kernels, on_device(): pl.pallas_call(inner_kernel, out_shape=(jax.ShapeDtypeStruct((heads, leng...  0.87 us
  transfers between devices with their start and end apart: 9, of which 7 were waited for; matrix products, arithmetic and copies ran while one was open for 0% of the time, Pallas kernels for 5%

profile of v4, /device:TPU:0, one launch (start us, length us, event | category | flops | bytes accessed | tf_op | source)
XLA Modules:
  0.0 39.9 jit_solution(1220188072390493350)
XLA Ops:
  0.0 1.4 %shard_map.56 = (f32[264,128]{1,0:T(8,128)S(1)}, f32[264,128]{1,0:T(8,128)S(1)}, f32[264,128]{1,0:T(8,128)S(1)}, f32[264,128]{1,0:T(8,128)S(1)}) custom-call(bf16[128,512]{1,0:T(8,128)(2,1)} %k_hbm.1, bf16[128,1024]{1,0:T(8,128)(2,1)} %v_hbm.1, f32[4,128]{1,0:T(4,128)} %in_hbm.1, f32[4,128]{1,0:T(4,128)} %fo_hbm.1), custom_call_target="tpu_custom_call" | custom-call | tf_op jit(solution)/shard_map/pallas_call | solution.py:364
  1.5 4.0 %collective-permute-start = (f32[264,128]{1,0:T(8,128)S(1)}, f32[264,128]{1,0:T(8,128)S(1)}, u32[]{:S(2)}, u32[]{:S(2)}) collective-permute-start(f32[264,128]{1,0:T(8,128)S(1)} %get-tuple-element.22), channel_id=1, source_target_pairs={{0,3},{1,2},{2,1},{3,0},{4,7},{5,6},{6,5},{7,4},{8,11},{9,10},{10,... | collective-permute-start | bytes 405512 | tf_op jit(solution)/shard_map/ppermute | solution.py:343
  5.5 0.4 %collective-permute-start.1 = (f32[264,128]{1,0:T(8,128)S(1)}, f32[264,128]{1,0:T(8,128)S(1)}, u32[]{:S(2)}, u32[]{:S(2)}) collective-permute-start(f32[264,128]{1,0:T(8,128)S(1)} %get-tuple-element.23), channel_id=1, source_target_pairs={{0,2},{1,3},{2,0},{3,1},{4,6},{5,7},{6,4},{7,5},{8,10},{9,11},{10,... | collective-permute-start | bytes 405512 | tf_op jit(solution)/shard_map/ppermute | solution.py:343
  5.9 0.2 collective-permute-start.2
  6.1 3.8 %collective-permute-done.refs_1_ = f32[264,128]{1,0:T(8,128)S(1)} collective-permute-done((f32[264,128]{1,0:T(8,128)S(1)}, f32[264,128]{1,0:T(8,128)S(1)}, u32[]{:S(2)}, u32[]{:S(2)}) %collective-permute-start) | collective-permute-done | bytes 135200 | tf_op jit(solution)/shard_map/ppermute | solution.py:343
  9.9 2.2 %collective-permute-done.1.refs_2_ = f32[264,128]{1,0:T(8,128)S(1)} collective-permute-done((f32[264,128]{1,0:T(8,128)S(1)}, f32[264,128]{1,0:T(8,128)S(1)}, u32[]{:S(2)}, u32[]{:S(2)}) %collective-permute-start.1) | collective-permute-done | bytes 135200 | tf_op jit(solution)/shard_map/ppermute | solution.py:343
  12.1 0.0 collective-permute-done.2.refs_3_
  12.1 0.1 shard_map.57.refs_0_
  12.2 2.7 %collective-permute-start.3 = (f32[264,128]{1,0:T(8,128)S(1)}, f32[264,128]{1,0:T(8,128)S(1)}, u32[]{:S(2)}, u32[]{:S(2)}) collective-permute-start(f32[264,128]{1,0:T(8,128)S(1)} %shard_map.57.refs_0_), channel_id=1, source_target_pairs={{0,4},{1,5},{2,6},{3,7},{4,0},{5,1},{6,2},{7,3},{8,12},{9,13},{10,... | collective-permute-start | bytes 405512 | tf_op jit(solution)/shard_map/ppermute | solution.py:343
  14.9 5.9 %collective-permute-done.3.refs_1_ = f32[264,128]{1,0:T(8,128)S(1)} collective-permute-done((f32[264,128]{1,0:T(8,128)S(1)}, f32[264,128]{1,0:T(8,128)S(1)}, u32[]{:S(2)}, u32[]{:S(2)}) %collective-permute-start.3) | collective-permute-done | bytes 135200 | tf_op jit(solution)/shard_map/ppermute | solution.py:343
  20.8 0.1 shard_map.58
  20.9 1.6 %collective-permute-start.4 = (f32[264,128]{1,0:T(8,128)S(1)}, f32[264,128]{1,0:T(8,128)S(1)}, u32[]{:S(2)}, u32[]{:S(2)}) collective-permute-start(f32[264,128]{1,0:T(8,128)S(1)} %get-tuple-element.25.own_ref), channel_id=1, source_target_pairs={{0,16},{8,24},{16,0},{24,8},{1,17},{9,25},{17,1},{25,9},{2,18},{10... | collective-permute-start | bytes 405512 | tf_op jit(solution)/shard_map/ppermute | solution.py:343
  22.5 3.5 %collective-permute-done.4.other_ref = f32[264,128]{1,0:T(8,128)S(1)} collective-permute-done((f32[264,128]{1,0:T(8,128)S(1)}, f32[264,128]{1,0:T(8,128)S(1)}, u32[]{:S(2)}, u32[]{:S(2)}) %collective-permute-start.4) | collective-permute-done | bytes 135200 | tf_op jit(solution)/shard_map/ppermute | solution.py:343
  26.0 0.1 collective-permute-start.5
  26.1 1.5 %collective-permute-done.5.other_ref = f32[2,264,128]{2,1,0:T(8,128)S(1)} collective-permute-done((f32[2,264,128]{2,1,0:T(8,128)S(1)}, f32[2,264,128]{2,1,0:T(8,128)S(1)}, u32[]{:S(2)}, u32[]{:S(2)}) %collective-permute-start.5) | collective-permute-done | bytes 270368 | tf_op jit(solution)/shard_map/ppermute | solution.py:343
  27.6 0.0 copy-start
  27.6 0.0 copy-start.1
  27.6 0.0 copy-start.2
  27.6 0.3 shard_map.60
  28.0 0.0 copy-start.4
  28.0 0.0 copy-start.3
  28.0 2.8 %collective-permute-start.8 = (f32[264,128]{1,0:T(8,128)S(1)}, f32[264,128]{1,0:T(8,128)S(1)}, u32[]{:S(2)}, u32[]{:S(2)}) collective-permute-start(f32[264,128]{1,0:T(8,128)S(1)} %get-tuple-element.31), channel_id=1, source_target_pairs={{0,3},{1,2},{2,1},{3,0},{4,7},{5,6},{6,5},{7,4},{8,11},{9,10},{10,... | collective-permute-start | bytes 405512 | tf_op jit(solution)/shard_map/ppermute | solution.py:343
  30.7 1.0 %collective-permute-start.7 = (f32[264,128]{1,0:T(8,128)S(1)}, f32[264,128]{1,0:T(8,128)S(1)}, u32[]{:S(2)}, u32[]{:S(2)}) collective-permute-start(f32[264,128]{1,0:T(8,128)S(1)} %get-tuple-element.29), channel_id=1, source_target_pairs={{0,2},{1,3},{2,0},{3,1},{4,6},{5,7},{6,4},{7,5},{8,10},{9,11},{10,... | collective-permute-start | bytes 405512 | tf_op jit(solution)/shard_map/ppermute | solution.py:343
  31.7 0.0 collective-permute-start.6
  31.7 0.0 copy-done
  31.7 0.0 copy-done.1
  31.7 0.0 copy-done.2
  31.7 0.0 copy-done.4
  31.8 0.0 copy-done.3
  31.8 0.9 %shard_map.55 = (f32[4,128,256]{2,1,0:T(8,128)S(1)}, f32[4,128,3]{2,1,0:T(8,128)S(1)}) custom-call(bf16[128,512]{1,0:T(8,128)(2,1)S(1)} %copy-done, bf16[128,512]{1,0:T(8,128)(2,1)S(1)} %copy-done.2, bf16[128,1024]{1,0:T(8,128)(2,1)S(1)} %copy-done.1, f32[4,128]{1,0:T(4,128)S(1)} %copy-done.3, f32[4,128]{1,0:T(4,128)S(1)} %copy-done.4), custom_call_target="tpu_custom_call" | custom-call | tf_op jit(solution)/shard_map/pallas_call | solution.py:373
  32.6 2.7 %collective-permute-done.8.refs_0_ = f32[264,128]{1,0:T(8,128)S(1)} collective-permute-done((f32[264,128]{1,0:T(8,128)S(1)}, f32[264,128]{1,0:T(8,128)S(1)}, u32[]{:S(2)}, u32[]{:S(2)}) %collective-permute-start.8) | collective-permute-done | bytes 135200 | tf_op jit(solution)/shard_map/ppermute | solution.py:343
  35.4 0.4 %shard_map.62.refs_1_ = bf16[128,256]{1,0:T(8,128)(2,1)S(1)} custom-call(bf16[128,512]{1,0:T(8,128)(2,1)S(1)} %copy-done, f32[4,128,256]{2,1,0:T(8,128)S(1)} %get-tuple-element.19.num_ref, f32[4,128,3]{2,1,0:T(8,128)S(1)} %get-tuple-element.20.stat_ref, f32[264,128]{1,0:T(8,128)S(1)} %collective-permute-done.8.refs_0_), custom_call_target="tpu_custom_call" | custom-call | tf_op jit(solution)/shard_map/pallas_call | solution.py:413
  35.8 2.5 %collective-permute-done.7.refs_1_ = f32[264,128]{1,0:T(8,128)S(1)} collective-permute-done((f32[264,128]{1,0:T(8,128)S(1)}, f32[264,128]{1,0:T(8,128)S(1)}, u32[]{:S(2)}, u32[]{:S(2)}) %collective-permute-start.7) | collective-permute-done | bytes 135200 | tf_op jit(solution)/shard_map/ppermute | solution.py:343
  38.3 0.6 %shard_map.61 = (bf16[128,256]{1,0:T(8,128)(2,1)S(1)}, bf16[128,256]{1,0:T(8,128)(2,1)S(1)}) custom-call(bf16[128,512]{1,0:T(8,128)(2,1)S(1)} %copy-done, f32[4,128,256]{2,1,0:T(8,128)S(1)} %get-tuple-element.19.num_ref, f32[4,128,3]{2,1,0:T(8,128)S(1)} %get-tuple-element.20.stat_ref, f32[264,128]{1,0:T(8,128)S(1)} %get-tuple-element.28.refs_0_, ...), custom_call_target="tpu_custom_call" | custom-call | tf_op jit(solution)/shard_map/pallas_call | solution.py:413
  38.8 0.0 collective-permute-done.6.message_ref
  38.8 1.1 %shard_map.63 = bf16[128,1024]{1,0:T(8,128)(2,1)} custom-call(bf16[128,512]{1,0:T(8,128)(2,1)S(1)} %copy-done, f32[4,128,256]{2,1,0:T(8,128)S(1)} %get-tuple-element.19.num_ref, f32[4,128,3]{2,1,0:T(8,128)S(1)} %get-tuple-element.20.stat_ref, f32[264,128]{1,0:T(8,128)S(1)} %collective-permute-done.6.message_ref, ...), custom_call_target="tpu_custom_call" | custom-call | tf_op jit(solution)/shard_map/pallas_call | solution.py:419
  (1 shorter events, 0.0 us)
Async XLA Ops:
  1.5 8.5 %collective-permute-start = (f32[264,128]{1,0:T(8,128)S(1)}, f32[264,128]{1,0:T(8,128)S(1)}, u32[]{:S(2)}, u32[]{:S(2)}) collective-permute-start(f32[264,128]{1,0:T(8,128)S(1)} %get-tuple-element.22), channel_id=1, source_target_pairs={{0,3},{1,2},{2,1},{3,0},{4,7},{5,6},{6,5},{7,4},{8,11},{9,10},{10,... | collective-permute-start | bytes 405512 | tf_op jit(solution)/shard_map/ppermute | solution.py:343
  5.5 6.6 %collective-permute-start.1 = (f32[264,128]{1,0:T(8,128)S(1)}, f32[264,128]{1,0:T(8,128)S(1)}, u32[]{:S(2)}, u32[]{:S(2)}) collective-permute-start(f32[264,128]{1,0:T(8,128)S(1)} %get-tuple-element.23), channel_id=1, source_target_pairs={{0,2},{1,3},{2,0},{3,1},{4,6},{5,7},{6,4},{7,5},{8,10},{9,11},{10,... | collective-permute-start | bytes 405512 | tf_op jit(solution)/shard_map/ppermute | solution.py:343
  5.9 6.2 %collective-permute-start.2 = (f32[264,128]{1,0:T(8,128)S(1)}, f32[264,128]{1,0:T(8,128)S(1)}, u32[]{:S(2)}, u32[]{:S(2)}) collective-permute-start(f32[264,128]{1,0:T(8,128)S(1)} %get-tuple-element.24), channel_id=1, source_target_pairs={{0,1},{1,0},{2,3},{3,2},{4,5},{5,4},{6,7},{7,6},{8,9},{9,8},{10,11... | collective-permute-start | bytes 405512 | tf_op jit(solution)/shard_map/ppermute | solution.py:343
  12.2 8.6 %collective-permute-start.3 = (f32[264,128]{1,0:T(8,128)S(1)}, f32[264,128]{1,0:T(8,128)S(1)}, u32[]{:S(2)}, u32[]{:S(2)}) collective-permute-start(f32[264,128]{1,0:T(8,128)S(1)} %shard_map.57.refs_0_), channel_id=1, source_target_pairs={{0,4},{1,5},{2,6},{3,7},{4,0},{5,1},{6,2},{7,3},{8,12},{9,13},{10,... | collective-permute-start | bytes 405512 | tf_op jit(solution)/shard_map/ppermute | solution.py:343
  20.9 5.1 %collective-permute-start.4 = (f32[264,128]{1,0:T(8,128)S(1)}, f32[264,128]{1,0:T(8,128)S(1)}, u32[]{:S(2)}, u32[]{:S(2)}) collective-permute-start(f32[264,128]{1,0:T(8,128)S(1)} %get-tuple-element.25.own_ref), channel_id=1, source_target_pairs={{0,16},{8,24},{16,0},{24,8},{1,17},{9,25},{17,1},{25,9},{2,18},{10... | collective-permute-start | bytes 405512 | tf_op jit(solution)/shard_map/ppermute | solution.py:343
  26.0 1.6 %collective-permute-start.5 = (f32[2,264,128]{2,1,0:T(8,128)S(1)}, f32[2,264,128]{2,1,0:T(8,128)S(1)}, u32[]{:S(2)}, u32[]{:S(2)}) collective-permute-start(f32[2,264,128]{2,1,0:T(8,128)S(1)} %shard_map.59.own_ref), channel_id=1, source_target_pairs={{0,8},{8,0},{16,24},{24,16},{1,9},{9,1},{17,25},{25,17},{2,10},{10... | collective-permute-start | bytes 811016 | tf_op jit(solution)/shard_map/ppermute | solution.py:343
  27.6 4.1 %copy-start = (bf16[128,512]{1,0:T(8,128)(2,1)S(1)}, bf16[128,512]{1,0:T(8,128)(2,1)}, u32[]{:S(2)}) copy-start(bf16[128,512]{1,0:T(8,128)(2,1)} %q_ref.7) | copy-start | bytes 393220
  27.6 4.1 %copy-start.1 = (bf16[128,1024]{1,0:T(8,128)(2,1)S(1)}, bf16[128,1024]{1,0:T(8,128)(2,1)}, u32[]{:S(2)}) copy-start(bf16[128,1024]{1,0:T(8,128)(2,1)} %v_hbm.1) | copy-start | bytes 786436
  27.6 4.1 %copy-start.2 = (bf16[128,512]{1,0:T(8,128)(2,1)S(1)}, bf16[128,512]{1,0:T(8,128)(2,1)}, u32[]{:S(2)}) copy-start(bf16[128,512]{1,0:T(8,128)(2,1)} %k_hbm.1) | copy-start | bytes 393220
  28.0 3.8 %copy-start.4 = (f32[4,128]{1,0:T(4,128)S(1)}, f32[4,128]{1,0:T(4,128)}, u32[]{:S(2)}) copy-start(f32[4,128]{1,0:T(4,128)} %fo_hbm.1) | copy-start | bytes 6148
  28.0 3.8 %copy-start.3 = (f32[4,128]{1,0:T(4,128)S(1)}, f32[4,128]{1,0:T(4,128)}, u32[]{:S(2)}) copy-start(f32[4,128]{1,0:T(4,128)} %in_hbm.1) | copy-start | bytes 6148
  28.0 7.4 %collective-permute-start.8 = (f32[264,128]{1,0:T(8,128)S(1)}, f32[264,128]{1,0:T(8,128)S(1)}, u32[]{:S(2)}, u32[]{:S(2)}) collective-permute-start(f32[264,128]{1,0:T(8,128)S(1)} %get-tuple-element.31), channel_id=1, source_target_pairs={{0,3},{1,2},{2,1},{3,0},{4,7},{5,6},{6,5},{7,4},{8,11},{9,10},{10,... | collective-permute-start | bytes 405512 | tf_op jit(solution)/shard_map/ppermute | solution.py:343
  30.7 7.5 %collective-permute-start.7 = (f32[264,128]{1,0:T(8,128)S(1)}, f32[264,128]{1,0:T(8,128)S(1)}, u32[]{:S(2)}, u32[]{:S(2)}) collective-permute-start(f32[264,128]{1,0:T(8,128)S(1)} %get-tuple-element.29), channel_id=1, source_target_pairs={{0,2},{1,3},{2,0},{3,1},{4,6},{5,7},{6,4},{7,5},{8,10},{9,11},{10,... | collective-permute-start | bytes 405512 | tf_op jit(solution)/shard_map/ppermute | solution.py:343
  31.7 7.1 %collective-permute-start.6 = (f32[264,128]{1,0:T(8,128)S(1)}, f32[264,128]{1,0:T(8,128)S(1)}, u32[]{:S(2)}, u32[]{:S(2)}) collective-permute-start(f32[264,128]{1,0:T(8,128)S(1)} %get-tuple-element.27), channel_id=1, source_target_pairs={{0,1},{1,0},{2,3},{3,2},{4,5},{5,4},{6,7},{7,6},{8,9},{9,8},{10,11... | collective-permute-start | bytes 405512 | tf_op jit(solution)/shard_map/ppermute | solution.py:343

commit v5 on v2

--- a/solution.py
+++ b/solution.py
@@ -44,10 +44,16 @@
     return rows >= cols if lower else rows <= cols
 
 
+def dot_exact(x, b):
+    count = x.shape[0]
+    terms = [term.astype(jnp.float32) for term in split_three(x)]
+    stacked = dot(jnp.concatenate(terms, axis=0).astype(jnp.bfloat16), b)
+    high, mid, low = (stacked[term * count : (term + 1) * count, :] for term in range(3))
+    return (low + mid) + high
+
+
 def cumulative_rows(logf):
-    ones = triangle(logf.shape[1], False).astype(jnp.bfloat16)
-    high, mid, low = split_three(logf)
-    return (dot(low, ones) + dot(mid, ones)) + dot(high, ones)
+    return dot_exact(logf, triangle(logf.shape[1], False).astype(jnp.bfloat16))
 
 
 def cumulative_columns(logf):
@@ -126,15 +132,17 @@
     key_dim = k_ref.shape[1] // heads
     value_dim = v_ref.shape[1] // heads
     parts = value_dim // LANES
-    for copy in copies:
-        copy.wait()
+    copies[0].wait()
     cumul = cumulative_rows(log_forget(fo_ref[...]))
+    copies[1].wait()
     level = in_ref[...] - cumul
     level_top = jnp.max(level, axis=1, keepdims=True)
     decay = cumul[:, length - 1 : length]
     scalar_ref[0] = jnp.exp(level - level_top)
     scalar_ref[1] = jnp.broadcast_to(decay + level_top, (heads, length))
     scalar_ref[2] = jnp.broadcast_to(decay, (heads, length))
+    copies[2].wait()
+    copies[3].wait()
     for head, out_ref in zip(partners(heads), out_refs):
         keys = k_ref[:, pl.ds(pl.multiple_of(head * key_dim, LANES), key_dim)]
         values = v_ref[:, pl.ds(pl.multiple_of(head * value_dim, LANES), value_dim)]
@@ -147,8 +155,7 @@
             out_ref[part * key_dim : (part + 1) * key_dim, :] = matrix[
                 :, part * LANES : (part + 1) * LANES
             ]
-        high, mid, low = split_three(row)
-        vector = (dot(low, keys) + dot(mid, keys)) + dot(high, keys)
+        vector = dot_exact(row, keys)
         out_ref[parts * key_dim :, :] = tail_rows(vector, top, decay)
 
 
@@ -401,14 +408,13 @@
     )(sums, swap(sums, AXES[0], 1), *within, *pieces)
     carried = exchange(states)
     column = jax.ShapeDtypeStruct((length, value_dim), output.dtype)
-    columns = {}
-    for steps in [(0, *range(2, heads - 1)), (1,)]:
-        outs = pl.pallas_call(
+    columns = []
+    for steps in [(0, 1)] + [(step,) for step in range(2, heads - 1)]:
+        columns += pl.pallas_call(
             functools.partial(part_kernel, steps),
             out_shape=(column,) * len(steps),
             compiler_params=params,
         )(queries, inner_num, stats, *(carried[step] for step in steps))
-        columns.update(zip(steps, outs))
     return pl.pallas_call(
         last_kernel,
         out_shape=output,
@@ -418,7 +424,7 @@
             pltpu.SemaphoreType.DMA((heads,)),
         ],
         compiler_params=params,
-    )(queries, inner_num, stats, carried[-1], *(columns[step] for step in range(heads - 1)))
+    )(queries, inner_num, stats, carried[-1], *columns)
 
 
 def solution(mesh):

time: 39.1 us -> 38 us (0.972)
  Pallas kernels: 5.09 us -> 4.48 us
  waiting for transfers between devices: 21.1 us -> 20.6 us
    ppermute x9, waiting for transfers between devices: 21.1 us -> 20.6 us  [swap(): lax.ppermute(array, axis, [(place, place ^ step) for place in range(count)])]
  transfers between devices with their start and end apart: 9 -> 9, of which waited for: 9 -> 8; matrix products, arithmetic and copies ran while one was open for 0% -> 0% of each run, Pallas kernels for 5% -> 4%
where the time goes in v5:
time: 38 us; the launch traced here: 37.9 us
  waiting for transfers between devices  20.6 us (54%)
  starting transfers between devices  12.6 us (33%)
  Pallas kernels  4.48 us (12%)
    ppermute x9, waiting for transfers between devices, swap(): lax.ppermute(array, axis, [(place, place ^ step) for place in range(count)])  20.6 us
    ppermute x9, starting transfers between devices, swap(): lax.ppermute(array, axis, [(place, place ^ step) for place in range(count)])  12.6 us
    pallas_call x1, Pallas kernels, on_device(): pl.pallas_call(state_kernel, out_shape=messages, in_specs=[hbm] * len(ope...  1.41 us
    pallas_call x1, Pallas kernels, on_device(): pl.pallas_call(last_kernel, out_shape=output, out_specs=hbm, scratch_shap...  1.08 us
    pallas_call x2, Pallas kernels, on_device(): pl.pallas_call(functools.partial(part_kernel, steps), out_shape=(column,)...  1.01 us
  transfers between devices with their start and end apart: 9, of which 8 were waited for; matrix products, arithmetic and copies ran while one was open for 0% of the time, Pallas kernels for 4%

profile of v5, /device:TPU:0, one launch (start us, length us, event | category | flops | bytes accessed | tf_op | source)
XLA Modules:
  0.0 37.9 jit_solution(15607742929524484734)
XLA Ops:
  0.0 1.4 %shard_map.56 = (f32[264,128]{1,0:T(8,128)S(1)}, f32[264,128]{1,0:T(8,128)S(1)}, f32[264,128]{1,0:T(8,128)S(1)}, f32[264,128]{1,0:T(8,128)S(1)}) custom-call(bf16[128,512]{1,0:T(8,128)(2,1)} %k_hbm.1, bf16[128,1024]{1,0:T(8,128)(2,1)} %v_hbm.1, f32[4,128]{1,0:T(4,128)} %in_hbm.1, f32[4,128]{1,0:T(4,128)} %fo_hbm.1), custom_call_target="tpu_custom_call" | custom-call | tf_op jit(solution)/shard_map/pallas_call | solution.py:364
  1.4 3.0 %collective-permute-start = (f32[264,128]{1,0:T(8,128)S(1)}, f32[264,128]{1,0:T(8,128)S(1)}, u32[]{:S(2)}, u32[]{:S(2)}) collective-permute-start(f32[264,128]{1,0:T(8,128)S(1)} %get-tuple-element.22), channel_id=1, source_target_pairs={{0,1},{1,0},{2,3},{3,2},{4,5},{5,4},{6,7},{7,6},{8,9},{9,8},{10,11... | collective-permute-start | bytes 405512 | tf_op jit(solution)/shard_map/ppermute | solution.py:344
  4.4 1.6 %collective-permute-start.1 = (f32[264,128]{1,0:T(8,128)S(1)}, f32[264,128]{1,0:T(8,128)S(1)}, u32[]{:S(2)}, u32[]{:S(2)}) collective-permute-start(f32[264,128]{1,0:T(8,128)S(1)} %get-tuple-element.23), channel_id=1, source_target_pairs={{0,2},{1,3},{2,0},{3,1},{4,6},{5,7},{6,4},{7,5},{8,10},{9,11},{10,... | collective-permute-start | bytes 405512 | tf_op jit(solution)/shard_map/ppermute | solution.py:344
  6.0 0.0 collective-permute-start.2
  6.0 2.0 %collective-permute-done.refs_1_ = f32[264,128]{1,0:T(8,128)S(1)} collective-permute-done((f32[264,128]{1,0:T(8,128)S(1)}, f32[264,128]{1,0:T(8,128)S(1)}, u32[]{:S(2)}, u32[]{:S(2)}) %collective-permute-start) | collective-permute-done | bytes 135200 | tf_op jit(solution)/shard_map/ppermute | solution.py:344
  8.0 2.9 %collective-permute-done.1.refs_2_ = f32[264,128]{1,0:T(8,128)S(1)} collective-permute-done((f32[264,128]{1,0:T(8,128)S(1)}, f32[264,128]{1,0:T(8,128)S(1)}, u32[]{:S(2)}, u32[]{:S(2)}) %collective-permute-start.1) | collective-permute-done | bytes 135200 | tf_op jit(solution)/shard_map/ppermute | solution.py:344
  10.9 1.2 %collective-permute-done.2.refs_3_ = f32[264,128]{1,0:T(8,128)S(1)} collective-permute-done((f32[264,128]{1,0:T(8,128)S(1)}, f32[264,128]{1,0:T(8,128)S(1)}, u32[]{:S(2)}, u32[]{:S(2)}) %collective-permute-start.2) | collective-permute-done | bytes 135200 | tf_op jit(solution)/shard_map/ppermute | solution.py:344
  12.2 0.1 shard_map.57.refs_0_
  12.3 2.8 %collective-permute-start.3 = (f32[264,128]{1,0:T(8,128)S(1)}, f32[264,128]{1,0:T(8,128)S(1)}, u32[]{:S(2)}, u32[]{:S(2)}) collective-permute-start(f32[264,128]{1,0:T(8,128)S(1)} %shard_map.57.refs_0_), channel_id=1, source_target_pairs={{0,4},{1,5},{2,6},{3,7},{4,0},{5,1},{6,2},{7,3},{8,12},{9,13},{10,... | collective-permute-start | bytes 405512 | tf_op jit(solution)/shard_map/ppermute | solution.py:344
  15.1 5.6 %collective-permute-done.3.refs_1_ = f32[264,128]{1,0:T(8,128)S(1)} collective-permute-done((f32[264,128]{1,0:T(8,128)S(1)}, f32[264,128]{1,0:T(8,128)S(1)}, u32[]{:S(2)}, u32[]{:S(2)}) %collective-permute-start.3) | collective-permute-done | bytes 135200 | tf_op jit(solution)/shard_map/ppermute | solution.py:344
  20.7 0.1 shard_map.58
  20.8 1.6 %collective-permute-start.4 = (f32[264,128]{1,0:T(8,128)S(1)}, f32[264,128]{1,0:T(8,128)S(1)}, u32[]{:S(2)}, u32[]{:S(2)}) collective-permute-start(f32[264,128]{1,0:T(8,128)S(1)} %get-tuple-element.25.own_ref), channel_id=1, source_target_pairs={{0,16},{8,24},{16,0},{24,8},{1,17},{9,25},{17,1},{25,9},{2,18},{10... | collective-permute-start | bytes 405512 | tf_op jit(solution)/shard_map/ppermute | solution.py:344
  22.4 3.5 %collective-permute-done.4.other_ref = f32[264,128]{1,0:T(8,128)S(1)} collective-permute-done((f32[264,128]{1,0:T(8,128)S(1)}, f32[264,128]{1,0:T(8,128)S(1)}, u32[]{:S(2)}, u32[]{:S(2)}) %collective-permute-start.4) | collective-permute-done | bytes 135200 | tf_op jit(solution)/shard_map/ppermute | solution.py:344
  25.9 0.1 collective-permute-start.5
  26.0 1.5 %collective-permute-done.5.other_ref = f32[2,264,128]{2,1,0:T(8,128)S(1)} collective-permute-done((f32[2,264,128]{2,1,0:T(8,128)S(1)}, f32[2,264,128]{2,1,0:T(8,128)S(1)}, u32[]{:S(2)}, u32[]{:S(2)}) %collective-permute-start.5) | collective-permute-done | bytes 270368 | tf_op jit(solution)/shard_map/ppermute | solution.py:344
  27.5 0.0 copy-start
  27.5 0.0 copy-start.1
  27.5 0.0 copy-start.2
  27.5 0.3 shard_map.60
  27.8 0.0 copy-start.4
  27.8 0.0 copy-start.3
  27.9 0.3 collective-permute-start.8
  28.1 1.4 %collective-permute-start.7 = (f32[264,128]{1,0:T(8,128)S(1)}, f32[264,128]{1,0:T(8,128)S(1)}, u32[]{:S(2)}, u32[]{:S(2)}) collective-permute-start(f32[264,128]{1,0:T(8,128)S(1)} %get-tuple-element.29), channel_id=1, source_target_pairs={{0,1},{1,0},{2,3},{3,2},{4,5},{5,4},{6,7},{7,6},{8,9},{9,8},{10,11... | collective-permute-start | bytes 405512 | tf_op jit(solution)/shard_map/ppermute | solution.py:344
  29.5 1.9 %collective-permute-start.6 = (f32[264,128]{1,0:T(8,128)S(1)}, f32[264,128]{1,0:T(8,128)S(1)}, u32[]{:S(2)}, u32[]{:S(2)}) collective-permute-start(f32[264,128]{1,0:T(8,128)S(1)} %get-tuple-element.27), channel_id=1, source_target_pairs={{0,3},{1,2},{2,1},{3,0},{4,7},{5,6},{6,5},{7,4},{8,11},{9,10},{10,... | collective-permute-start | bytes 405512 | tf_op jit(solution)/shard_map/ppermute | solution.py:344
  31.4 0.0 copy-done
  31.4 0.0 copy-done.1
  31.4 0.0 copy-done.2
  31.4 0.0 copy-done.4
  31.4 0.0 copy-done.3
  31.4 0.5 %shard_map.55 = (f32[4,128,256]{2,1,0:T(8,128)S(1)}, f32[4,128,3]{2,1,0:T(8,128)S(1)}) custom-call(bf16[128,512]{1,0:T(8,128)(2,1)S(1)} %copy-done, bf16[128,512]{1,0:T(8,128)(2,1)S(1)} %copy-done.2, bf16[128,1024]{1,0:T(8,128)(2,1)S(1)} %copy-done.1, f32[4,128]{1,0:T(4,128)S(1)} %copy-done.3, f32[4,128]{1,0:T(4,128)S(1)} %copy-done.4), custom_call_target="tpu_custom_call" | custom-call | tf_op jit(solution)/shard_map/pallas_call | solution.py:373
  31.9 2.4 %collective-permute-done.8.refs_0_ = f32[264,128]{1,0:T(8,128)S(1)} collective-permute-done((f32[264,128]{1,0:T(8,128)S(1)}, f32[264,128]{1,0:T(8,128)S(1)}, u32[]{:S(2)}, u32[]{:S(2)}) %collective-permute-start.8) | collective-permute-done | bytes 135200 | tf_op jit(solution)/shard_map/ppermute | solution.py:344
  34.3 0.4 %shard_map.62.refs_2_ = bf16[128,256]{1,0:T(8,128)(2,1)S(1)} custom-call(bf16[128,512]{1,0:T(8,128)(2,1)S(1)} %copy-done, f32[4,128,256]{2,1,0:T(8,128)S(1)} %get-tuple-element.19.num_ref, f32[4,128,3]{2,1,0:T(8,128)S(1)} %get-tuple-element.20.stat_ref, f32[264,128]{1,0:T(8,128)S(1)} %collective-permute-done.8.refs_0_), custom_call_target="tpu_custom_call" | custom-call | tf_op jit(solution)/shard_map/pallas_call | solution.py:413
  34.8 0.0 collective-permute-done.7.refs_1_
  34.8 0.6 %shard_map.61 = (bf16[128,256]{1,0:T(8,128)(2,1)S(1)}, bf16[128,256]{1,0:T(8,128)(2,1)S(1)}) custom-call(bf16[128,512]{1,0:T(8,128)(2,1)S(1)} %copy-done, f32[4,128,256]{2,1,0:T(8,128)S(1)} %get-tuple-element.19.num_ref, f32[4,128,3]{2,1,0:T(8,128)S(1)} %get-tuple-element.20.stat_ref, f32[264,128]{1,0:T(8,128)S(1)} %get-tuple-element.28.refs_0_, ...), custom_call_target="tpu_custom_call" | custom-call | tf_op jit(solution)/shard_map/pallas_call | solution.py:413
  35.4 1.4 %collective-permute-done.6.message_ref = f32[264,128]{1,0:T(8,128)S(1)} collective-permute-done((f32[264,128]{1,0:T(8,128)S(1)}, f32[264,128]{1,0:T(8,128)S(1)}, u32[]{:S(2)}, u32[]{:S(2)}) %collective-permute-start.6) | collective-permute-done | bytes 135200 | tf_op jit(solution)/shard_map/ppermute | solution.py:344
  36.8 1.1 %shard_map.63 = bf16[128,1024]{1,0:T(8,128)(2,1)} custom-call(bf16[128,512]{1,0:T(8,128)(2,1)S(1)} %copy-done, f32[4,128,256]{2,1,0:T(8,128)S(1)} %get-tuple-element.19.num_ref, f32[4,128,3]{2,1,0:T(8,128)S(1)} %get-tuple-element.20.stat_ref, f32[264,128]{1,0:T(8,128)S(1)} %collective-permute-done.6.message_ref, ...), custom_call_target="tpu_custom_call" | custom-call | tf_op jit(solution)/shard_map/pallas_call | solution.py:418
  (1 shorter events, 0.0 us)
Async XLA Ops:
  1.4 6.6 %collective-permute-start = (f32[264,128]{1,0:T(8,128)S(1)}, f32[264,128]{1,0:T(8,128)S(1)}, u32[]{:S(2)}, u32[]{:S(2)}) collective-permute-start(f32[264,128]{1,0:T(8,128)S(1)} %get-tuple-element.22), channel_id=1, source_target_pairs={{0,1},{1,0},{2,3},{3,2},{4,5},{5,4},{6,7},{7,6},{8,9},{9,8},{10,11... | collective-permute-start | bytes 405512 | tf_op jit(solution)/shard_map/ppermute | solution.py:344
  4.4 6.5 %collective-permute-start.1 = (f32[264,128]{1,0:T(8,128)S(1)}, f32[264,128]{1,0:T(8,128)S(1)}, u32[]{:S(2)}, u32[]{:S(2)}) collective-permute-start(f32[264,128]{1,0:T(8,128)S(1)} %get-tuple-element.23), channel_id=1, source_target_pairs={{0,2},{1,3},{2,0},{3,1},{4,6},{5,7},{6,4},{7,5},{8,10},{9,11},{10,... | collective-permute-start | bytes 405512 | tf_op jit(solution)/shard_map/ppermute | solution.py:344
  6.0 6.2 %collective-permute-start.2 = (f32[264,128]{1,0:T(8,128)S(1)}, f32[264,128]{1,0:T(8,128)S(1)}, u32[]{:S(2)}, u32[]{:S(2)}) collective-permute-start(f32[264,128]{1,0:T(8,128)S(1)} %get-tuple-element.24), channel_id=1, source_target_pairs={{0,3},{1,2},{2,1},{3,0},{4,7},{5,6},{6,5},{7,4},{8,11},{9,10},{10,... | collective-permute-start | bytes 405512 | tf_op jit(solution)/shard_map/ppermute | solution.py:344
  12.3 8.4 %collective-permute-start.3 = (f32[264,128]{1,0:T(8,128)S(1)}, f32[264,128]{1,0:T(8,128)S(1)}, u32[]{:S(2)}, u32[]{:S(2)}) collective-permute-start(f32[264,128]{1,0:T(8,128)S(1)} %shard_map.57.refs_0_), channel_id=1, source_target_pairs={{0,4},{1,5},{2,6},{3,7},{4,0},{5,1},{6,2},{7,3},{8,12},{9,13},{10,... | collective-permute-start | bytes 405512 | tf_op jit(solution)/shard_map/ppermute | solution.py:344
  20.8 5.1 %collective-permute-start.4 = (f32[264,128]{1,0:T(8,128)S(1)}, f32[264,128]{1,0:T(8,128)S(1)}, u32[]{:S(2)}, u32[]{:S(2)}) collective-permute-start(f32[264,128]{1,0:T(8,128)S(1)} %get-tuple-element.25.own_ref), channel_id=1, source_target_pairs={{0,16},{8,24},{16,0},{24,8},{1,17},{9,25},{17,1},{25,9},{2,18},{10... | collective-permute-start | bytes 405512 | tf_op jit(solution)/shard_map/ppermute | solution.py:344
  25.9 1.6 %collective-permute-start.5 = (f32[2,264,128]{2,1,0:T(8,128)S(1)}, f32[2,264,128]{2,1,0:T(8,128)S(1)}, u32[]{:S(2)}, u32[]{:S(2)}) collective-permute-start(f32[2,264,128]{2,1,0:T(8,128)S(1)} %shard_map.59.own_ref), channel_id=1, source_target_pairs={{0,8},{8,0},{16,24},{24,16},{1,9},{9,1},{17,25},{25,17},{2,10},{10... | collective-permute-start | bytes 811016 | tf_op jit(solution)/shard_map/ppermute | solution.py:344
  27.5 3.9 %copy-start = (bf16[128,512]{1,0:T(8,128)(2,1)S(1)}, bf16[128,512]{1,0:T(8,128)(2,1)}, u32[]{:S(2)}) copy-start(bf16[128,512]{1,0:T(8,128)(2,1)} %q_ref.7) | copy-start | bytes 393220
  27.5 3.9 %copy-start.1 = (bf16[128,1024]{1,0:T(8,128)(2,1)S(1)}, bf16[128,1024]{1,0:T(8,128)(2,1)}, u32[]{:S(2)}) copy-start(bf16[128,1024]{1,0:T(8,128)(2,1)} %v_hbm.1) | copy-start | bytes 786436
  27.5 3.9 %copy-start.2 = (bf16[128,512]{1,0:T(8,128)(2,1)S(1)}, bf16[128,512]{1,0:T(8,128)(2,1)}, u32[]{:S(2)}) copy-start(bf16[128,512]{1,0:T(8,128)(2,1)} %k_hbm.1) | copy-start | bytes 393220
  27.8 3.6 %copy-start.4 = (f32[4,128]{1,0:T(4,128)S(1)}, f32[4,128]{1,0:T(4,128)}, u32[]{:S(2)}) copy-start(f32[4,128]{1,0:T(4,128)} %fo_hbm.1) | copy-start | bytes 6148
  27.8 3.6 %copy-start.3 = (f32[4,128]{1,0:T(4,128)S(1)}, f32[4,128]{1,0:T(4,128)}, u32[]{:S(2)}) copy-start(f32[4,128]{1,0:T(4,128)} %in_hbm.1) | copy-start | bytes 6148
  27.9 6.5 %collective-permute-start.8 = (f32[264,128]{1,0:T(8,128)S(1)}, f32[264,128]{1,0:T(8,128)S(1)}, u32[]{:S(2)}, u32[]{:S(2)}) collective-permute-start(f32[264,128]{1,0:T(8,128)S(1)} %get-tuple-element.32), channel_id=1, source_target_pairs={{0,2},{1,3},{2,0},{3,1},{4,6},{5,7},{6,4},{7,5},{8,10},{9,11},{10,... | collective-permute-start | bytes 405512 | tf_op jit(solution)/shard_map/ppermute | solution.py:344
  28.1 6.6 %collective-permute-start.7 = (f32[264,128]{1,0:T(8,128)S(1)}, f32[264,128]{1,0:T(8,128)S(1)}, u32[]{:S(2)}, u32[]{:S(2)}) collective-permute-start(f32[264,128]{1,0:T(8,128)S(1)} %get-tuple-element.29), channel_id=1, source_target_pairs={{0,1},{1,0},{2,3},{3,2},{4,5},{5,4},{6,7},{7,6},{8,9},{9,8},{10,11... | collective-permute-start | bytes 405512 | tf_op jit(solution)/shard_map/ppermute | solution.py:344
  29.5 7.3 %collective-permute-start.6 = (f32[264,128]{1,0:T(8,128)S(1)}, f32[264,128]{1,0:T(8,128)S(1)}, u32[]{:S(2)}, u32[]{:S(2)}) collective-permute-start(f32[264,128]{1,0:T(8,128)S(1)} %get-tuple-element.27), channel_id=1, source_target_pairs={{0,3},{1,2},{2,1},{3,0},{4,7},{5,6},{6,5},{7,4},{8,11},{9,10},{10,... | collective-permute-start | bytes 405512 | tf_op jit(solution)/shard_map/ppermute | solution.py:344
